TPU v7x, 32 devices: a whole 2x2x4 slice. The times are simulated.
32 devices in a mesh: groups: 2 (over y), pool: 16 (over z, x, core).
Axes of the slice: x: 2, y: 2, z: 4, core: 2. Of those that a mesh axis runs over, the one named last changes fastest.
Arguments:
- queries: bfloat16 [128, 6144], P(('groups', 'pool')), parts along dimension 0, may hold values from -70 to 70
- keys_cache: bfloat16 [128, 192, 1024], P(('groups', 'pool')), parts along dimension 0, may hold values from -3 to 3
- values_cache: bfloat16 [128, 192, 1024], P(('groups', 'pool')), parts along dimension 0, may hold values from -6 to 6
- lengths: int32 [128], P(('groups', 'pool')), parts along dimension 0, may hold values from 1 to 192, 6144 in all
- hidden: bfloat16 [128, 6144], P(('groups', 'pool')), parts along dimension 0, may hold values from -6 to 6
- norm_gain: bfloat16 [6144], replicated, may hold values from 0.25 to 1.75
- expert_ids: int32 [128, 2], P(('groups', 'pool')), parts along dimension 0, may hold values from 0 to 3, all different within a row; in each aligned block of 4 rows (0 to 3, 4 to 7, ...) at most 3 rows name the same one
- gate_weights: bfloat16 [128, 2], P(('groups', 'pool')), parts along dimension 0, may hold values from 0.25 to 1
- w_gate: bfloat16 [6144, 32768], P(None, 'pool'), may hold values from -0.078125 to 0.078125
- w_up: bfloat16 [6144, 32768], P(None, 'pool'), may hold values from -0.078125 to 0.078125
- w_down: bfloat16 [32768, 6144], P('pool'), may hold values from -0.0625 to 0.0625
Outputs:
- context: bfloat16 [128, 6144], P(('groups', 'pool')), parts along dimension 0
- moe_out: bfloat16 [128, 6144], P(('groups', 'pool')), parts along dimension 0
There are 2 independent parts, one for each index of `groups`. A program takes and returns all parts, laid end to end along the dimension named above; an argument that names none is the same for every part. Nothing has to cross between parts.
Inputs may be any that keep to these rules, and one draw needn't show every extreme that they name: `expert_ids`: the two ids of a row differ. Among the 4 rows of one device (aligned blocks of rows), no expert is named by more than 3 rows, and in some blocks one expert is named by exactly 3; every expert is named somewhere. `lengths`: some row has all 192 slots live.
All inputs are finite; a program needn't handle non-finite values. No bound on the sum of `lengths` on one device may be relied on, other than what follows from the above.
Results may differ from a plain program's by a relative error of at most 0.0044.
Values may be sent and summed in bfloat16 or wider, within the bound.
No kernel may reach another device: no remote copies, remote signals or barrier semaphores. Data moves between devices by JAX's collectives and lax.ppermute only.
A program may use at most 192 MiB of HBM per device.

v0:
```python
import jax
import jax.numpy as jnp
from jax import lax
from jax.sharding import PartitionSpec as P

EXPERTS = 4
HEADS = 48
KV_HEADS = 8
HEAD_DIM = 128
CAP = 3


EPS = 1e-05


def normalize(hidden, norm_gain):
    values = hidden.astype(jnp.float32)
    row_scale = lax.rsqrt(jnp.mean(values * values, axis=-1, keepdims=True) + EPS)
    return (values * row_scale * norm_gain.astype(jnp.float32)).astype(jnp.bfloat16)


def expert_ffn(normed, w_gate, w_up, w_down):
    gate_proj = jnp.dot(normed, w_gate, preferred_element_type=jnp.float32)
    up_proj = jnp.dot(normed, w_up, preferred_element_type=jnp.float32)
    active = (jax.nn.silu(gate_proj) * up_proj).astype(jnp.bfloat16)
    return jnp.dot(active, w_down, preferred_element_type=jnp.float32)


def attend(queries, keys_cache, values_cache, lengths):
    row_count = queries.shape[0]
    cache_span = keys_cache.shape[1]
    query_heads = queries.reshape(row_count, KV_HEADS, HEADS // KV_HEADS, HEAD_DIM)
    key_heads = keys_cache.reshape(row_count, cache_span, KV_HEADS, HEAD_DIM)
    value_heads = values_cache.reshape(row_count, cache_span, KV_HEADS, HEAD_DIM)
    scores = jnp.einsum(
        "rkgd,rlkd->rkgl", query_heads, key_heads, preferred_element_type=jnp.float32
    ) * HEAD_DIM ** (-0.5)
    live_mask = (
        jnp.arange(cache_span, dtype=jnp.int32)[None, None, None, :] < lengths[:, None, None, None]
    )
    scores = jnp.where(live_mask, scores, -jnp.inf)
    row_max = jnp.max(scores, axis=-1, keepdims=True)
    raised = jnp.exp(scores - row_max)
    row_total = jnp.sum(raised, axis=-1, keepdims=True)
    attn_weights = (raised / row_total).astype(jnp.bfloat16)
    context = jnp.einsum(
        "rkgl,rlkd->rkgd", attn_weights, value_heads, preferred_element_type=jnp.float32
    )
    return context.reshape(row_count, HEADS * HEAD_DIM).astype(jnp.bfloat16)


def local(
    queries,
    keys_cache,
    values_cache,
    lengths,
    hidden,
    norm_gain,
    expert_ids,
    gate_weights,
    w_gate,
    w_up,
    w_down,
):
    normed = normalize(hidden, norm_gain)
    devices = lax.axis_size("pool")
    group_size = devices // EXPERTS
    expert_range = jnp.arange(EXPERTS, dtype=jnp.int32)
    picked = expert_ids[:, :, None] == expert_range[None, None, :]
    coefficient = jnp.sum(
        jnp.where(picked, gate_weights[:, :, None].astype(jnp.float32), 0.0), axis=1
    )
    chosen = jnp.any(picked, axis=1)
    taken_count = chosen.astype(jnp.int32)
    slot_index = jnp.cumsum(taken_count, axis=0) - taken_count
    slot_mask = chosen[:, :, None] & (
        slot_index[:, :, None] == jnp.arange(CAP, dtype=jnp.int32)[None, None, :]
    )
    slot_onehot = slot_mask.astype(jnp.bfloat16)
    outgoing = jnp.einsum(
        "rec,rd->ecd", slot_onehot, normed, preferred_element_type=jnp.float32
    ).astype(jnp.bfloat16)
    outgoing = jnp.repeat(outgoing, group_size, axis=0)
    incoming = lax.all_to_all(outgoing, "pool", split_axis=0, concat_axis=0, tiled=True)
    sources, slot_count, model_width = incoming.shape
    partial_value = expert_ffn(
        incoming.reshape(sources * slot_count, model_width), w_gate, w_up, w_down
    )
    partial_value = partial_value.reshape(sources, slot_count, model_width)
    returned = lax.all_to_all(partial_value, "pool", split_axis=0, concat_axis=0, tiled=True)
    summed = jnp.sum(
        returned.reshape(EXPERTS, group_size, returned.shape[1], returned.shape[2]), axis=1
    )
    spread = jnp.where(slot_mask, coefficient[:, :, None], 0.0)
    mixture = jnp.einsum("rec,ecd->rd", spread, summed, precision=lax.Precision.HIGHEST)
    moe_out = (hidden.astype(jnp.float32) + mixture).astype(jnp.bfloat16)
    context = attend(queries, keys_cache, values_cache, lengths)
    return (context, moe_out)


def solution(mesh):
    return jax.shard_map(
        local,
        mesh=mesh,
        in_specs=(
            P(("groups", "pool"), None),
            P(("groups", "pool"), None, None),
            P(("groups", "pool"), None, None),
            P(("groups", "pool")),
            P(("groups", "pool"), None),
            P(),
            P(("groups", "pool"), None),
            P(("groups", "pool"), None),
            P(None, "pool"),
            P(None, "pool"),
            P("pool", None),
        ),
        out_specs=(P(("groups", "pool"), None), P(("groups", "pool"), None)),
        check_vma=False,
    )
```

profile of v0, /device:TPU:15, one launch (start us, length us, event | category | flops | bytes accessed | tf_op | source)
XLA Modules:
  0.0 106.5 jit_solution(8481686417609327668)
XLA Ops:
  0.6 0.0 copy-start
  0.6 0.9 fusion.39
  1.6 0.7 convert_element_type.50
  2.3 1.0 fusion.30
  3.3 1.1 %convolution_convert_fusion = bf16[4,3,6144]{2,0,1:T(4,128)(2,1)S(1)} fusion(bf16[4,6144]{1,0:T(4,128)(2,1)} %param.15, f32[6144]{0:T(1024)S(1)} %convert_element_type.50, f32[4]{0:T(128)S(1)} %add_rsqrt_fusion, s32[4,4]{1,0:T(4,128)S(1)} %convert_subtract_fusion, pred[4,4]{1,0:T(4,128)(4,1)S(1)} %fusion.39), kind=kOutput, calls=%fused_computation.1 | convolution fusion | flops 761952 | bytes 221280 | tf_op jit(solution)/shard_map/rec,rd->ecd/dot_general | solution.py:80
  4.4 0.1 copy.35
  4.5 0.3 broadcast_in_dim.58
  4.8 25.6 %all_to_all.10 = bf16[16,3,6144]{2,1,0:T(4,128)(2,1)S(1)} all-to-all(bf16[16,3,6144]{2,1,0:T(4,128)(2,1)S(1)} %bitcast.40), channel_id=1, replica_groups=mesh['groups'=2,'pool'=16] {'pool'}, dimensions={0} | all-to-all | bytes 1179648 | tf_op jit(solution)/shard_map/all_to_all | solution.py:84
  30.4 0.5 reshape.80
  30.9 11.2 %fusion.51 = f32[48,2048]{1,0:T(8,128)} fusion(bf16[48,6144]{1,0:T(8,128)(2,1)S(1)} %reshape.80, bf16[6144,2048]{1,0:T(8,128)(2,1)} %param.19), kind=kOutput, calls=%fused_computation.55 | convolution fusion | flops 1207959552 | bytes 26148864 | tf_op jit(solution)/shard_map/dot_general | solution.py:23
  42.1 20.0 %fusion.4 = f32[48,6144]{1,0:T(8,128)S(1)} fusion(bf16[2048,6144]{1,0:T(8,128)(2,1)} %param.21, bf16[48,6144]{1,0:T(8,128)(2,1)S(1)} %reshape.80, bf16[6144,2048]{1,0:T(8,128)(2,1)} %param.20, f32[48,2048]{1,0:T(8,128)} %fusion.51), kind=kOutput, calls=%fused_computation.7 | convolution fusion | flops 2416508928 | bytes 52494336 | tf_op jit(solution)/shard_map/dot_general | solution.py:26
  62.1 1.4 %reshape.81 = f32[16,3,6144]{2,1,0:T(4,128)} reshape(f32[48,6144]{1,0:T(8,128)S(1)} %fusion.4) | data formatting | bytes 2359296 | tf_op jit(solution)/shard_map/reshape | solution.py:89
  63.6 0.0 copy-start.4
  63.6 0.0 copy-start.2
  63.6 0.0 copy-start.5
  63.6 5.1 %all-to-all-start.1 = ((f32[16,3,6144]{2,1,0:T(4,128)}), f32[16,3,6144]{2,1,0:T(4,128)S(1)}, u32[]{:S(2)}, u32[]{:S(2)}) async-start(f32[16,3,6144]{2,1,0:T(4,128)} %reshape.81), calls=%async_computation.1 | async-start | bytes 3145728 | tf_op jit(solution)/shard_map/all_to_all | solution.py:90
  68.7 0.0 copy-done.4
  68.7 0.0 copy-done.2
  68.7 0.1 reshape.76
  68.8 0.0 copy-done.5
  68.8 0.1 iota_compare_fusion.2
  68.9 0.0 copy-done
  68.9 0.9 fusion.15
  69.8 0.0 copy-start.3
  69.8 0.2 fusion.50
  70.0 2.0 %fusion.19 = bf16[4,8,6,128]{3,2,1,0:T(8,128)(2,1)S(1)} fusion(f32[4,8,6]{2,1,0:T(8,128)S(1)} %fusion.50, f32[4,8,6,192]{3,2,1,0:T(8,128)S(1)} %fusion.15, bf16[4,192,1024]{2,1,0:T(8,128)(2,1)} %param.13), kind=kOutput, calls=%fused_computation.19 | convolution fusion | flops 9572735 | bytes 1770240 | tf_op jit(solution)/shard_map/rkgl,rlkd->rkgd/dot_general | solution.py:46
  72.0 0.0 copy-start.1
  72.0 0.7 convert_element_type.46
  72.7 0.0 copy-done.3
  72.7 0.1 select_reduce_fusion
  72.8 32.1 %all-to-all-done.1 = f32[16,3,6144]{2,1,0:T(4,128)S(1)} async-done(((f32[16,3,6144]{2,1,0:T(4,128)}), f32[16,3,6144]{2,1,0:T(4,128)S(1)}, u32[]{:S(2)}, u32[]{:S(2)}) %all-to-all-start.1) | async-done | bytes 1179680 | tf_op jit(solution)/shard_map/all_to_all | solution.py:90
  104.9 0.2 bitcast_reduce_fusion
  105.1 0.0 copy-done.1
  105.1 1.4 %fusion.2 = bf16[4,6144]{1,0:T(4,128)(2,1)} fusion(f32[4,3,6144]{2,1,0:T(4,128)S(1)} %bitcast_reduce_fusion, bf16[4,6144]{1,0:T(4,128)(2,1)S(1)} %copy-done.1, f32[4,4]{1,0:T(4,128)S(1)} %select_reduce_fusion, s32[4,4]{1,0:T(4,128)S(1)} %convert_subtract_fusion, pred[4,4]{1,0:T(4,128)(4,1)S(1)} %fusion.39), kind=kOutput, calls=%fused_computation.4 | convolution fusion | flops 3612816 | bytes 393360 | tf_op jit(solution)/shard_map/rec,ecd->rd/dot_general | solution.py:95
  (5 shorter events, 0.1 us)
Async XLA Ops:
  0.6 68.3 %copy-start = (bf16[4,192,1024]{2,1,0:T(8,128)(2,1)S(1)}, bf16[4,192,1024]{2,1,0:T(8,128)(2,1)}, u32[]{:S(2)}) copy-start(bf16[4,192,1024]{2,1,0:T(8,128)(2,1)} %param.12) | copy-start | bytes 4718596
  63.6 5.1 %copy-start.4 = (bf16[4,2]{0,1:T(2,128)(2,1)S(1)}, bf16[4,2]{0,1:T(2,128)(2,1)}, u32[]{:S(2)}) copy-start(bf16[4,2]{0,1:T(2,128)(2,1)} %param.18) | copy-start | bytes 52
  63.6 5.1 %copy-start.2 = (bf16[4,6144]{1,0:T(4,128)(2,1)S(1)}, bf16[4,6144]{1,0:T(4,128)(2,1)}, u32[]{:S(2)}) copy-start(bf16[4,6144]{1,0:T(4,128)(2,1)} %param.11) | copy-start | bytes 147460
  63.6 5.2 %copy-start.5 = (s32[4]{0:T(128)S(1)}, s32[4]{0:T(128)}, u32[]{:S(2)}) copy-start(s32[4]{0:T(128)} %param.14) | copy-start | bytes 52
  63.6 41.3 %all-to-all-start.1 = ((f32[16,3,6144]{2,1,0:T(4,128)}), f32[16,3,6144]{2,1,0:T(4,128)S(1)}, u32[]{:S(2)}, u32[]{:S(2)}) async-start(f32[16,3,6144]{2,1,0:T(4,128)} %reshape.81), calls=%async_computation.1 | async-start | bytes 3145728 | tf_op jit(solution)/shard_map/all_to_all | solution.py:90
  69.8 2.9 %copy-start.3 = (s32[4,2]{0,1:T(2,128)S(1)}, s32[4,2]{0,1:T(2,128)}, u32[]{:S(2)}) copy-start(s32[4,2]{0,1:T(2,128)} %param.17) | copy-start | bytes 100
  72.0 33.1 %copy-start.1 = (bf16[4,6144]{1,0:T(4,128)(2,1)S(1)}, bf16[4,6144]{1,0:T(4,128)(2,1)}, u32[]{:S(2)}) copy-start(bf16[4,6144]{1,0:T(4,128)(2,1)} %param.15) | copy-start | bytes 147460
where the time goes:
time: 107 us; the launch traced here: 106 us
  matrix products  36.6 us (34%)
  waiting for transfers between devices  32.1 us (30%)
  blocking collectives  25.6 us (24%)
  starting transfers between devices  5.11 us (5%)
  other arithmetic  3.24 us (3%)
  local copies, waits for them, and re-layouts  3.15 us (3%)
    all_to_all x1, waiting for transfers between devices, local(): lax.all_to_all(partial_value, 'pool', split_axis=0, concat_axis=0, tiled=...  32.1 us
    all_to_all x1, blocking collectives, local(): lax.all_to_all(outgoing, 'pool', split_axis=0, concat_axis=0, tiled=True)  25.6 us
    dot_general x1, matrix products, expert_ffn(): return jnp.dot(active, w_down, preferred_element_type=jnp.float32)  20 us
    dot_general x1, matrix products, expert_ffn(): gate_proj = jnp.dot(normed, w_gate, preferred_element_type=jnp.float32)  11.2 us
    all_to_all x1, starting transfers between devices, local(): lax.all_to_all(partial_value, 'pool', split_axis=0, concat_axis=0, tiled=...  5.11 us
  transfers between devices with their start and end apart: 1, of which 1 were waited for; matrix products, arithmetic and copies ran while one was open for 4% of the time, Pallas kernels for 0%

commit v1 on v0

v1 whole, which is shorter than its diff:
```python
import functools

import jax
import jax.numpy as jnp
from jax import lax
from jax.experimental import pallas as pl
from jax.experimental.pallas import tpu as pltpu
from jax.sharding import PartitionSpec as P

EXPERTS = 4
HEADS = 48
KV_HEADS = 8
HEAD_DIM = 128
EPS = 1e-05
MIB = 1 << 20


def norm_kernel(hidden_ref, gain_ref, normed_ref):
    values = hidden_ref[...].astype(jnp.float32)
    row_scale = lax.rsqrt(jnp.mean(values * values, axis=-1, keepdims=True) + EPS)
    normed_ref[...] = (values * row_scale * gain_ref[...].astype(jnp.float32)).astype(jnp.bfloat16)


def normalize(hidden, norm_gain):
    return pl.pallas_call(
        norm_kernel,
        out_shape=jax.ShapeDtypeStruct(hidden.shape, jnp.bfloat16),
        compiler_params=pltpu.CompilerParams(vmem_limit_bytes=8 * MIB),
    )(hidden, norm_gain.reshape(1, -1))


def ffn_kernel(
    depth, width, x_ref, gate_hbm, up_hbm, down_hbm, keep_ref, send_ref,
    gate_buf, up_buf, down_buf, gate_sum, up_sum, active, gate_sem, up_sem, down_sem,
):
    ring = gate_buf.shape[0]
    down_ring = down_buf.shape[0]
    steps = gate_hbm.shape[0] // depth
    down_steps = down_hbm.shape[1] // width
    half = keep_ref.shape[0]

    def gate_copy(step, slot):
        rows = pl.ds(pl.multiple_of(step * depth, depth), depth)
        return pltpu.make_async_copy(gate_hbm.at[rows, :], gate_buf.at[slot], gate_sem.at[slot])

    def up_copy(step, slot):
        rows = pl.ds(pl.multiple_of(step * depth, depth), depth)
        return pltpu.make_async_copy(up_hbm.at[rows, :], up_buf.at[slot], up_sem.at[slot])

    def down_copy(step, slot):
        columns = pl.ds(pl.multiple_of(step * width, width), width)
        return pltpu.make_async_copy(
            down_hbm.at[:, columns], down_buf.at[slot], down_sem.at[slot]
        )

    for step in range(min(ring, steps)):
        gate_copy(step, step).start()
        up_copy(step, step).start()
    for step in range(min(down_ring, down_steps)):
        down_copy(step, step).start()
    gate_sum[...] = jnp.zeros_like(gate_sum)
    up_sum[...] = jnp.zeros_like(up_sum)

    @pl.loop(0, steps)
    def _(step):
        slot = lax.rem(step, ring)
        block = x_ref[:, pl.ds(pl.multiple_of(step * depth, depth), depth)]
        gate_copy(step, slot).wait()
        gate_sum[...] += jnp.dot(block, gate_buf[slot], preferred_element_type=jnp.float32)
        up_copy(step, slot).wait()
        up_sum[...] += jnp.dot(block, up_buf[slot], preferred_element_type=jnp.float32)

        @pl.when(step + ring < steps)
        def _():
            gate_copy(step + ring, slot).start()
            up_copy(step + ring, slot).start()

    gate_proj = gate_sum[...]
    active[...] = (gate_proj / (1.0 + jnp.exp(-gate_proj)) * up_sum[...]).astype(jnp.bfloat16)

    @pl.loop(0, down_steps)
    def _(step):
        slot = lax.rem(step, down_ring)
        columns = pl.ds(pl.multiple_of(step * width, width), width)
        down_copy(step, slot).wait()
        out = jnp.dot(active[...], down_buf[slot], preferred_element_type=jnp.float32)
        keep_ref[:, columns] = out[:half]
        send_ref[:, columns] = out[half:].astype(jnp.bfloat16)

        @pl.when(step + down_ring < down_steps)
        def _():
            down_copy(step + down_ring, slot).start()


def expert_ffn(x, w_gate, w_up, w_down):
    rows, model_width = x.shape
    units = w_gate.shape[1]
    depth = 1024
    width = 1024
    ring = 3
    down_ring = 3
    hbm = pl.BlockSpec(memory_space=pl.ANY)
    vmem = pl.BlockSpec(memory_space=pltpu.VMEM)
    return pl.pallas_call(
        functools.partial(ffn_kernel, depth, width),
        out_shape=(
            jax.ShapeDtypeStruct((rows // 2, model_width), jnp.float32),
            jax.ShapeDtypeStruct((rows // 2, model_width), jnp.bfloat16),
        ),
        in_specs=[vmem, hbm, hbm, hbm],
        out_specs=(vmem, vmem),
        scratch_shapes=[
            pltpu.VMEM((ring, depth, units), jnp.bfloat16),
            pltpu.VMEM((ring, depth, units), jnp.bfloat16),
            pltpu.VMEM((down_ring, units, width), jnp.bfloat16),
            pltpu.VMEM((rows, units), jnp.float32),
            pltpu.VMEM((rows, units), jnp.float32),
            pltpu.VMEM((rows, units), jnp.bfloat16),
            pltpu.SemaphoreType.DMA((ring,)),
            pltpu.SemaphoreType.DMA((ring,)),
            pltpu.SemaphoreType.DMA((down_ring,)),
        ],
        compiler_params=pltpu.CompilerParams(vmem_limit_bytes=50 * MIB),
        cost_estimate=pl.CostEstimate(
            flops=6 * rows * model_width * units,
            bytes_accessed=6 * model_width * units,
            transcendentals=rows * units,
        ),
    )(x, w_gate, w_up, w_down)


def attend(queries, keys_cache, values_cache, lengths):
    row_count = queries.shape[0]
    cache_span = keys_cache.shape[1]
    query_heads = queries.reshape(row_count, KV_HEADS, HEADS // KV_HEADS, HEAD_DIM)
    key_heads = keys_cache.reshape(row_count, cache_span, KV_HEADS, HEAD_DIM)
    value_heads = values_cache.reshape(row_count, cache_span, KV_HEADS, HEAD_DIM)
    scores = jnp.einsum(
        "rkgd,rlkd->rkgl", query_heads, key_heads, preferred_element_type=jnp.float32
    ) * HEAD_DIM ** (-0.5)
    live_mask = (
        jnp.arange(cache_span, dtype=jnp.int32)[None, None, None, :] < lengths[:, None, None, None]
    )
    scores = jnp.where(live_mask, scores, -jnp.inf)
    row_max = jnp.max(scores, axis=-1, keepdims=True)
    raised = jnp.exp(scores - row_max)
    row_total = jnp.sum(raised, axis=-1, keepdims=True)
    attn_weights = (raised / row_total).astype(jnp.bfloat16)
    context = jnp.einsum(
        "rkgl,rlkd->rkgd", attn_weights, value_heads, preferred_element_type=jnp.float32
    )
    return context.reshape(row_count, HEADS * HEAD_DIM).astype(jnp.bfloat16)


def local(
    queries,
    keys_cache,
    values_cache,
    lengths,
    hidden,
    norm_gain,
    expert_ids,
    gate_weights,
    w_gate,
    w_up,
    w_down,
):
    devices = lax.axis_size("pool")
    group_size = devices // EXPERTS
    own_rows = hidden.shape[0]

    def swap(value, distance):
        return lax.ppermute(value, "pool", [(i, i ^ distance) for i in range(devices)])

    near = []
    distance = 1
    while distance < group_size:
        near.append(distance)
        distance *= 2

    normed = normalize(hidden, norm_gain)
    x = jnp.concatenate(
        [normed] + [swap(normed, k * group_size) for k in range(1, EXPERTS)], axis=0
    )
    for distance in reversed(near):
        x = jnp.concatenate([x, swap(x, distance)], axis=0)

    keep, send = expert_ffn(x, w_gate, w_up, w_down)
    for at, distance in enumerate(near):
        total = keep + swap(send, distance).astype(jnp.float32)
        if at + 1 < len(near):
            half = total.shape[0] // 2
            keep, send = total[:half], total[half:].astype(jnp.bfloat16)

    own_expert = lax.axis_index("pool") // group_size
    mixture = jnp.zeros(hidden.shape, jnp.float32)
    for k in range(EXPERTS):
        block = total[k * own_rows : (k + 1) * own_rows]
        if k > 0:
            block = swap(block.astype(jnp.bfloat16), k * group_size).astype(jnp.float32)
        named = expert_ids == (own_expert ^ k)
        coefficient = jnp.sum(
            jnp.where(named, gate_weights.astype(jnp.float32), 0.0), axis=1, keepdims=True
        )
        mixture = mixture + coefficient * block
    moe_out = (hidden.astype(jnp.float32) + mixture).astype(jnp.bfloat16)
    context = attend(queries, keys_cache, values_cache, lengths)
    return (context, moe_out)


def solution(mesh):
    return jax.shard_map(
        local,
        mesh=mesh,
        in_specs=(
            P(("groups", "pool"), None),
            P(("groups", "pool"), None, None),
            P(("groups", "pool"), None, None),
            P(("groups", "pool")),
            P(("groups", "pool"), None),
            P(),
            P(("groups", "pool"), None),
            P(("groups", "pool"), None),
            P(None, "pool"),
            P(None, "pool"),
            P("pool", None),
        ),
        out_specs=(P(("groups", "pool"), None), P(("groups", "pool"), None)),
        check_vma=False,
    )
```

time: 107 us -> 66.6 us (0.62)
  the two profiles are of different devices: /device:TPU:15 before, /device:TPU:0 now
where the time goes in v1:
time: 66.6 us; the launch traced here: 66.3 us
  Pallas kernels  26.8 us (40%)
  waiting for transfers between devices  16.2 us (24%)
  starting transfers between devices  13.8 us (21%)
  local copies, waits for them, and re-layouts  3.85 us (6%)
  matrix products  2.88 us (4%)
  other arithmetic  1.98 us (3%)
  between operations  0.78 us (1%)
    pallas_call x1, Pallas kernels, expert_ffn(): pl.pallas_call(functools.partial(ffn_kernel, depth, width), out_shape=(ja...  26.7 us
    ppermute x10, waiting for transfers between devices, swap(): lax.ppermute(value, 'pool', [(i, i ^ distance) for i in range(devices)])  16.2 us
    ppermute x10, starting transfers between devices, swap(): lax.ppermute(value, 'pool', [(i, i ^ distance) for i in range(devices)])  13.8 us
    dot_general x1, matrix products, attend(): jnp.einsum('rkgl,rlkd->rkgd', attn_weights, value_heads, preferred_elemen...  1.98 us
  transfers between devices with their start and end apart: 10, of which 8 were waited for; matrix products, arithmetic and copies ran while one was open for 8% of the time, Pallas kernels for 0%

profile of v1, /device:TPU:0, one launch (start us, length us, event | category | flops | bytes accessed | tf_op | source)
XLA Modules:
  0.0 66.3 jit_solution(11750290638316770928)
XLA Ops:
  0.6 0.0 copy-start
  0.6 0.8 %reshape.48.gain_ref = bf16[1,6144]{1,0:T(2,128)(2,1)S(1)} reshape(bf16[6144]{0:T(1024)(128)(2,1)} %param.16) | data formatting | bytes 24576 | tf_op jit(solution)/shard_map/reshape | solution.py:29
  1.5 0.0 copy-start.1
  1.5 0.8 %copy-done.1 = bf16[4,6144]{1,0:T(4,128)(2,1)S(1)} copy-done((bf16[4,6144]{1,0:T(4,128)(2,1)S(1)}, bf16[4,6144]{1,0:T(4,128)(2,1)}, u32[]{:S(2)}) %copy-start.1) | copy-done | bytes 49176
  2.3 0.2 shard_map.122
  2.5 3.1 %collective-permute-start = (bf16[4,6144]{1,0:T(4,128)(2,1)S(1)}, bf16[4,6144]{1,0:T(4,128)(2,1)S(1)}, u32[]{:S(2)}, u32[]{:S(2)}) collective-permute-start(bf16[4,6144]{1,0:T(4,128)(2,1)S(1)} %shard_map.122), channel_id=1, source_target_pairs={{0,4},{1,5},{2,6},{3,7},{4,0},{5,1},{6,2},{7,3},{8,12},{9,13},{10,... | collective-permute-start | bytes 147464 | tf_op jit(solution)/shard_map/ppermute | solution.py:173
  5.5 2.6 %collective-permute-start.1 = (bf16[4,6144]{1,0:T(4,128)(2,1)S(1)}, bf16[4,6144]{1,0:T(4,128)(2,1)S(1)}, u32[]{:S(2)}, u32[]{:S(2)}) collective-permute-start(bf16[4,6144]{1,0:T(4,128)(2,1)S(1)} %shard_map.122), channel_id=1, source_target_pairs={{0,8},{1,9},{2,10},{3,11},{4,12},{5,13},{6,14},{7,15},{8,0},{9,1},... | collective-permute-start | bytes 147464 | tf_op jit(solution)/shard_map/ppermute | solution.py:173
  8.1 0.0 collective-permute-start.2
  8.1 0.0 collective-permute-done
  8.1 3.3 %collective-permute-done.1 = bf16[4,6144]{1,0:T(4,128)(2,1)S(1)} collective-permute-done((bf16[4,6144]{1,0:T(4,128)(2,1)S(1)}, bf16[4,6144]{1,0:T(4,128)(2,1)S(1)}, u32[]{:S(2)}, u32[]{:S(2)}) %collective-permute-start.1) | collective-permute-done | bytes 49184 | tf_op jit(solution)/shard_map/ppermute | solution.py:173
  11.5 2.6 %collective-permute-done.2 = bf16[4,6144]{1,0:T(4,128)(2,1)S(1)} collective-permute-done((bf16[4,6144]{1,0:T(4,128)(2,1)S(1)}, bf16[4,6144]{1,0:T(4,128)(2,1)S(1)}, u32[]{:S(2)}, u32[]{:S(2)}) %collective-permute-start.2) | collective-permute-done | bytes 49184 | tf_op jit(solution)/shard_map/ppermute | solution.py:173
  14.0 0.1 pad_maximum_fusion
  14.1 1.6 %collective-permute-start.3 = (bf16[16,6144]{1,0:T(8,128)(2,1)S(1)}, bf16[16,6144]{1,0:T(8,128)(2,1)S(1)}, u32[]{:S(2)}, u32[]{:S(2)}) collective-permute-start(bf16[16,6144]{1,0:T(8,128)(2,1)S(1)} %pad_maximum_fusion), channel_id=1, source_target_pairs={{0,2},{1,3},{2,0},{3,1},{4,6},{5,7},{6,4},{7,5},{8,10},{9,11},{10,... | collective-permute-start | bytes 589832 | tf_op jit(solution)/shard_map/ppermute | solution.py:173
  15.7 4.2 %collective-permute-done.3 = bf16[16,6144]{1,0:T(8,128)(2,1)S(1)} collective-permute-done((bf16[16,6144]{1,0:T(8,128)(2,1)S(1)}, bf16[16,6144]{1,0:T(8,128)(2,1)S(1)}, u32[]{:S(2)}, u32[]{:S(2)}) %collective-permute-start.3) | collective-permute-done | bytes 196640 | tf_op jit(solution)/shard_map/ppermute | solution.py:173
  19.9 0.2 concatenate.12
  20.1 0.1 collective-permute-start.4
  20.2 0.9 %reshape.45 = bf16[4,8,6,128]{3,2,1,0:T(8,128)(2,1)S(1)} reshape(bf16[4,6144]{1,0:T(4,128)(2,1)} %param.11) | data formatting | bytes 98304 | tf_op jit(solution)/shard_map/reshape | solution.py:135
  21.1 0.7 %iota_compare_fusion = pred[4,192]{1,0:T(4,128)(4,1)S(1)} fusion(s32[4]{0:T(128)} %param.14), kind=kLoop, calls=%fused_computation.24 | loop fusion | flops 768 | bytes 784 | tf_op jit(solution)/shard_map/lt | solution.py:142
  21.8 0.1 collective-permute-done.4
  21.9 0.4 concatenate.13.x_ref
  22.3 26.7 %shard_map.123 = (f32[32,6144]{1,0:T(8,128)S(1)}, bf16[32,6144]{1,0:T(8,128)(2,1)S(1)}) custom-call(bf16[64,6144]{1,0:T(8,128)(2,1)S(1)} %concatenate.13.x_ref, bf16[6144,2048]{1,0:T(8,128)(2,1)} %gate_hbm.1, bf16[6144,2048]{1,0:T(8,128)(2,1)} %up_hbm.1, bf16[2048,6144]{1,0:T(8,128)(2,1)} %down_hbm.1), custom_call_target="tpu_custom_call" | custom-call | flops 4831838208 | bytes 75497472 | tf_op jit(solution)/shard_map/pallas_call | solution.py:104
  48.9 0.5 collective-permute-start.5
  49.4 0.0 copy-done
  49.4 0.9 %fusion.11 = f32[4,8,6,192]{3,2,1,0:T(8,128)S(1)} fusion(bf16[4,8,6,128]{3,2,1,0:T(8,128)(2,1)S(1)} %reshape.45, pred[4,192]{1,0:T(4,128)(4,1)S(1)} %iota_compare_fusion, bf16[4,192,1024]{2,1,0:T(8,128)(2,1)S(1)} %copy-done), kind=kOutput, calls=%fused_computation.9 | convolution fusion | flops 9510912 | bytes 1770240 | tf_op jit(solution)/shard_map/rkgd,rlkd->rkgl/dot_general | solution.py:138
  50.3 0.2 fusion.30
  50.5 0.2 collective-permute-done.5
  50.7 0.1 convert_add_fusion
  50.8 0.0 copy-start.3
  50.8 0.0 copy-start.4
  50.9 0.0 copy-start.2
  50.9 1.6 %collective-permute-start.6 = (bf16[16,6144]{1,0:T(8,128)(2,1)S(1)}, bf16[16,6144]{1,0:T(8,128)(2,1)S(1)}, u32[]{:S(2)}, u32[]{:S(2)}) collective-permute-start(bf16[16,6144]{1,0:T(8,128)(2,1)S(1)} %slice.47), channel_id=1, source_target_pairs={{0,2},{1,3},{2,0},{3,1},{4,6},{5,7},{6,4},{7,5},{8,10},{9,11},{10,... | collective-permute-start | bytes 589832 | tf_op jit(solution)/shard_map/ppermute | solution.py:173
  52.4 2.0 %fusion.15 = bf16[4,8,6,128]{3,2,1,0:T(8,128)(2,1)S(1)} fusion(f32[4,8,6]{2,1,0:T(8,128)S(1)} %fusion.30, f32[4,8,6,192]{3,2,1,0:T(8,128)S(1)} %fusion.11, bf16[4,192,1024]{2,1,0:T(8,128)(2,1)} %param.13), kind=kOutput, calls=%fused_computation.11 | convolution fusion | flops 9572735 | bytes 1770240 | tf_op jit(solution)/shard_map/rkgl,rlkd->rkgd/dot_general | solution.py:149
  54.4 3.7 %collective-permute-done.6 = bf16[16,6144]{1,0:T(8,128)(2,1)S(1)} collective-permute-done((bf16[16,6144]{1,0:T(8,128)(2,1)S(1)}, bf16[16,6144]{1,0:T(8,128)(2,1)S(1)}, u32[]{:S(2)}, u32[]{:S(2)}) %collective-permute-start.6) | collective-permute-done | bytes 196640 | tf_op jit(solution)/shard_map/ppermute | solution.py:173
  58.2 0.1 fusion.29
  58.2 0.1 collective-permute-start.7
  58.3 1.3 %collective-permute-start.8 = (bf16[4,6144]{1,0:T(4,128)(2,1)S(1)}, bf16[4,6144]{1,0:T(4,128)(2,1)S(1)}, u32[]{:S(2)}, u32[]{:S(2)}) collective-permute-start(bf16[4,6144]{1,0:T(4,128)(2,1)S(1)} %get-tuple-element.14), channel_id=1, source_target_pairs={{0,8},{1,9},{2,10},{3,11},{4,12},{5,13},{6,14},{7,15},{8,0},{9,1},... | collective-permute-start | bytes 147464 | tf_op jit(solution)/shard_map/ppermute | solution.py:173
  59.6 3.1 %collective-permute-start.9 = (bf16[4,6144]{1,0:T(4,128)(2,1)S(1)}, bf16[4,6144]{1,0:T(4,128)(2,1)S(1)}, u32[]{:S(2)}, u32[]{:S(2)}) collective-permute-start(bf16[4,6144]{1,0:T(4,128)(2,1)S(1)} %get-tuple-element.13), channel_id=1, source_target_pairs={{0,12},{1,13},{2,14},{3,15},{4,8},{5,9},{6,10},{7,11},{8,4},{9,5},... | collective-permute-start | bytes 147464 | tf_op jit(solution)/shard_map/ppermute | solution.py:173
  62.7 0.0 copy-done.3
  62.7 0.0 copy-done.4
  62.7 0.7 convert_element_type.42
  63.4 0.0 collective-permute-done.7
  63.4 0.7 %collective-permute-done.8 = bf16[4,6144]{1,0:T(4,128)(2,1)S(1)} collective-permute-done((bf16[4,6144]{1,0:T(4,128)(2,1)S(1)}, bf16[4,6144]{1,0:T(4,128)(2,1)S(1)}, u32[]{:S(2)}, u32[]{:S(2)}) %collective-permute-start.8) | collective-permute-done | bytes 49184 | tf_op jit(solution)/shard_map/ppermute | solution.py:173
  64.1 1.4 %collective-permute-done.9 = bf16[4,6144]{1,0:T(4,128)(2,1)S(1)} collective-permute-done((bf16[4,6144]{1,0:T(4,128)(2,1)S(1)}, bf16[4,6144]{1,0:T(4,128)(2,1)S(1)}, u32[]{:S(2)}, u32[]{:S(2)}) %collective-permute-start.9) | collective-permute-done | bytes 49184 | tf_op jit(solution)/shard_map/ppermute | solution.py:173
  65.5 0.0 copy-done.2
  65.5 0.8 %fusion.23 = bf16[4,6144]{1,0:T(4,128)(2,1)} fusion(f32[16,6144]{1,0:T(8,128)S(1)} %get-tuple-element.11, bf16[4,6144]{1,0:T(4,128)(2,1)S(1)} %collective-permute-done.9, bf16[4,6144]{1,0:T(4,128)(2,1)S(1)} %collective-permute-done.8, bf16[4,6144]{1,0:T(4,128)(2,1)S(1)} %collective-permute-done.7, bf16[4,6144]{1,0:T(4,128)(2,1)S(1)} %copy-done.2, ...), kind=kLoop, calls=%fused_computation.23 | loop fusion | flops 319488 | bytes 344128 | tf_op jit(solution)/shard_map/convert_element_type | solution.py:206
  (3 shorter events, 0.1 us)
Async XLA Ops:
  0.6 48.8 %copy-start = (bf16[4,192,1024]{2,1,0:T(8,128)(2,1)S(1)}, bf16[4,192,1024]{2,1,0:T(8,128)(2,1)}, u32[]{:S(2)}) copy-start(bf16[4,192,1024]{2,1,0:T(8,128)(2,1)} %param.12) | copy-start | bytes 4718596
  1.5 0.8 %copy-start.1 = (bf16[4,6144]{1,0:T(4,128)(2,1)S(1)}, bf16[4,6144]{1,0:T(4,128)(2,1)}, u32[]{:S(2)}) copy-start(bf16[4,6144]{1,0:T(4,128)(2,1)} %hidden_ref.1) | copy-start | bytes 147460
  2.5 5.7 %collective-permute-start = (bf16[4,6144]{1,0:T(4,128)(2,1)S(1)}, bf16[4,6144]{1,0:T(4,128)(2,1)S(1)}, u32[]{:S(2)}, u32[]{:S(2)}) collective-permute-start(bf16[4,6144]{1,0:T(4,128)(2,1)S(1)} %shard_map.122), channel_id=1, source_target_pairs={{0,4},{1,5},{2,6},{3,7},{4,0},{5,1},{6,2},{7,3},{8,12},{9,13},{10,... | collective-permute-start | bytes 147464 | tf_op jit(solution)/shard_map/ppermute | solution.py:173
  5.5 5.9 %collective-permute-start.1 = (bf16[4,6144]{1,0:T(4,128)(2,1)S(1)}, bf16[4,6144]{1,0:T(4,128)(2,1)S(1)}, u32[]{:S(2)}, u32[]{:S(2)}) collective-permute-start(bf16[4,6144]{1,0:T(4,128)(2,1)S(1)} %shard_map.122), channel_id=1, source_target_pairs={{0,8},{1,9},{2,10},{3,11},{4,12},{5,13},{6,14},{7,15},{8,0},{9,1},... | collective-permute-start | bytes 147464 | tf_op jit(solution)/shard_map/ppermute | solution.py:173
  8.1 5.9 %collective-permute-start.2 = (bf16[4,6144]{1,0:T(4,128)(2,1)S(1)}, bf16[4,6144]{1,0:T(4,128)(2,1)S(1)}, u32[]{:S(2)}, u32[]{:S(2)}) collective-permute-start(bf16[4,6144]{1,0:T(4,128)(2,1)S(1)} %shard_map.122), channel_id=1, source_target_pairs={{0,12},{1,13},{2,14},{3,15},{4,8},{5,9},{6,10},{7,11},{8,4},{9,5},... | collective-permute-start | bytes 147464 | tf_op jit(solution)/shard_map/ppermute | solution.py:173
  14.1 5.7 %collective-permute-start.3 = (bf16[16,6144]{1,0:T(8,128)(2,1)S(1)}, bf16[16,6144]{1,0:T(8,128)(2,1)S(1)}, u32[]{:S(2)}, u32[]{:S(2)}) collective-permute-start(bf16[16,6144]{1,0:T(8,128)(2,1)S(1)} %pad_maximum_fusion), channel_id=1, source_target_pairs={{0,2},{1,3},{2,0},{3,1},{4,6},{5,7},{6,4},{7,5},{8,10},{9,11},{10,... | collective-permute-start | bytes 589832 | tf_op jit(solution)/shard_map/ppermute | solution.py:173
  20.1 1.8 %collective-permute-start.4 = (bf16[32,6144]{1,0:T(8,128)(2,1)S(1)}, bf16[32,6144]{1,0:T(8,128)(2,1)S(1)}, u32[]{:S(2)}, u32[]{:S(2)}) collective-permute-start(bf16[32,6144]{1,0:T(8,128)(2,1)S(1)} %concatenate.12), channel_id=1, source_target_pairs={{0,1},{1,0},{2,3},{3,2},{4,5},{5,4},{6,7},{7,6},{8,9},{9,8},{10,11... | collective-permute-start | bytes 1179656 | tf_op jit(solution)/shard_map/ppermute | solution.py:173
  48.9 1.8 %collective-permute-start.5 = (bf16[32,6144]{1,0:T(8,128)(2,1)S(1)}, bf16[32,6144]{1,0:T(8,128)(2,1)S(1)}, u32[]{:S(2)}, u32[]{:S(2)}) collective-permute-start(bf16[32,6144]{1,0:T(8,128)(2,1)S(1)} %get-tuple-element.5), channel_id=1, source_target_pairs={{0,1},{1,0},{2,3},{3,2},{4,5},{5,4},{6,7},{7,6},{8,9},{9,8},{10,11... | collective-permute-start | bytes 1179656 | tf_op jit(solution)/shard_map/ppermute | solution.py:173
  50.8 11.9 %copy-start.3 = (s32[4,2]{0,1:T(2,128)S(1)}, s32[4,2]{0,1:T(2,128)}, u32[]{:S(2)}) copy-start(s32[4,2]{0,1:T(2,128)} %param.17) | copy-start | bytes 100
  50.8 11.8 %copy-start.4 = (bf16[4,2]{0,1:T(2,128)(2,1)S(1)}, bf16[4,2]{0,1:T(2,128)(2,1)}, u32[]{:S(2)}) copy-start(bf16[4,2]{0,1:T(2,128)(2,1)} %param.18) | copy-start | bytes 52
  50.9 14.7 %copy-start.2 = (bf16[4,6144]{1,0:T(4,128)(2,1)S(1)}, bf16[4,6144]{1,0:T(4,128)(2,1)}, u32[]{:S(2)}) copy-start(bf16[4,6144]{1,0:T(4,128)(2,1)} %hidden_ref.1) | copy-start | bytes 147460
  50.9 7.2 %collective-permute-start.6 = (bf16[16,6144]{1,0:T(8,128)(2,1)S(1)}, bf16[16,6144]{1,0:T(8,128)(2,1)S(1)}, u32[]{:S(2)}, u32[]{:S(2)}) collective-permute-start(bf16[16,6144]{1,0:T(8,128)(2,1)S(1)} %slice.47), channel_id=1, source_target_pairs={{0,2},{1,3},{2,0},{3,1},{4,6},{5,7},{6,4},{7,5},{8,10},{9,11},{10,... | collective-permute-start | bytes 589832 | tf_op jit(solution)/shard_map/ppermute | solution.py:173
  58.2 5.1 %collective-permute-start.7 = (bf16[4,6144]{1,0:T(4,128)(2,1)S(1)}, bf16[4,6144]{1,0:T(4,128)(2,1)S(1)}, u32[]{:S(2)}, u32[]{:S(2)}) collective-permute-start(bf16[4,6144]{1,0:T(4,128)(2,1)S(1)} %get-tuple-element.12), channel_id=1, source_target_pairs={{0,4},{1,5},{2,6},{3,7},{4,0},{5,1},{6,2},{7,3},{8,12},{9,13},{10,... | collective-permute-start | bytes 147464 | tf_op jit(solution)/shard_map/ppermute | solution.py:173
  58.3 5.8 %collective-permute-start.8 = (bf16[4,6144]{1,0:T(4,128)(2,1)S(1)}, bf16[4,6144]{1,0:T(4,128)(2,1)S(1)}, u32[]{:S(2)}, u32[]{:S(2)}) collective-permute-start(bf16[4,6144]{1,0:T(4,128)(2,1)S(1)} %get-tuple-element.14), channel_id=1, source_target_pairs={{0,8},{1,9},{2,10},{3,11},{4,12},{5,13},{6,14},{7,15},{8,0},{9,1},... | collective-permute-start | bytes 147464 | tf_op jit(solution)/shard_map/ppermute | solution.py:173
  59.6 5.9 %collective-permute-start.9 = (bf16[4,6144]{1,0:T(4,128)(2,1)S(1)}, bf16[4,6144]{1,0:T(4,128)(2,1)S(1)}, u32[]{:S(2)}, u32[]{:S(2)}) collective-permute-start(bf16[4,6144]{1,0:T(4,128)(2,1)S(1)} %get-tuple-element.13), channel_id=1, source_target_pairs={{0,12},{1,13},{2,14},{3,15},{4,8},{5,9},{6,10},{7,11},{8,4},{9,5},... | collective-permute-start | bytes 147464 | tf_op jit(solution)/shard_map/ppermute | solution.py:173

commit v2 on v1

v2 whole, which is shorter than its diff:
```python
import functools

import jax
import jax.numpy as jnp
from jax import lax
from jax.experimental import pallas as pl
from jax.experimental.pallas import tpu as pltpu
from jax.sharding import PartitionSpec as P

EXPERTS = 4
HEADS = 48
KV_HEADS = 8
HEAD_DIM = 128
EPS = 1e-05
MIB = 1 << 20
HBM = pl.BlockSpec(memory_space=pl.ANY)
VMEM = pl.BlockSpec(memory_space=pltpu.VMEM)
SMEM = pl.BlockSpec(memory_space=pltpu.SMEM)


def norm_kernel(hidden_hbm, gain_hbm, normed_ref, hidden_ref, gain_ref, sems):
    hidden_copy = pltpu.make_async_copy(hidden_hbm, hidden_ref, sems.at[0])
    gain_copy = pltpu.make_async_copy(gain_hbm, gain_ref, sems.at[1])
    hidden_copy.start()
    gain_copy.start()
    hidden_copy.wait()
    values = hidden_ref[...].astype(jnp.float32)
    row_scale = lax.rsqrt(jnp.mean(values * values, axis=-1, keepdims=True) + EPS)
    gain_copy.wait()
    gain = gain_ref[...].astype(jnp.float32).reshape(1, -1)
    normed_ref[...] = (values * row_scale * gain).astype(jnp.bfloat16)


def normalize(hidden, norm_gain):
    return pl.pallas_call(
        norm_kernel,
        out_shape=jax.ShapeDtypeStruct(hidden.shape, jnp.bfloat16),
        in_specs=[HBM, HBM],
        out_specs=VMEM,
        scratch_shapes=[
            pltpu.VMEM(hidden.shape, hidden.dtype),
            pltpu.VMEM(norm_gain.shape, norm_gain.dtype),
            pltpu.SemaphoreType.DMA((2,)),
        ],
        compiler_params=pltpu.CompilerParams(vmem_limit_bytes=60 * MIB),
    )(hidden, norm_gain)


def merge_kernel(count, *refs):
    merged_ref = refs[-1]
    merged_ref[...] = jnp.concatenate([ref[...] for ref in refs[:count]], axis=0)


def merge(blocks, after):
    rows = sum(block.shape[0] for block in blocks)
    return pl.pallas_call(
        functools.partial(merge_kernel, len(blocks)),
        in_specs=[VMEM] * (len(blocks) + len(after)),
        out_specs=VMEM,
        out_shape=jax.ShapeDtypeStruct((rows, blocks[0].shape[1]), blocks[0].dtype),
        compiler_params=pltpu.CompilerParams(vmem_limit_bytes=4 * MIB),
    )(*blocks, *after)


def prefetch_kernel(firsts, *refs):
    count = len(firsts)
    sources, targets, sems = refs[:count], refs[count + 1 : 2 * count + 1], refs[-1]
    copies = [
        pltpu.make_async_copy(source.at[pl.ds(first, target.shape[0]), :], target, sems.at[i])
        for i, (source, first, target) in enumerate(zip(sources, firsts, targets))
    ]
    for copy in copies:
        copy.start()
    for copy in copies:
        copy.wait()


def prefetch(parts, after, limit):
    total = sum(count * weights.shape[1] for weights, _, count in parts)
    return pl.pallas_call(
        functools.partial(prefetch_kernel, tuple(first for _, first, _ in parts)),
        out_shape=tuple(
            pltpu.VMEM((count, weights.shape[1]), weights.dtype) for weights, _, count in parts
        ),
        in_specs=[HBM] * len(parts) + [HBM],
        out_specs=(VMEM,) * len(parts),
        scratch_shapes=[pltpu.SemaphoreType.DMA((len(parts),))],
        compiler_params=pltpu.CompilerParams(vmem_limit_bytes=limit * MIB),
        cost_estimate=pl.CostEstimate(flops=0, bytes_accessed=2 * total, transcendentals=0),
    )(*[weights for weights, _, _ in parts], after)


def ffn_kernel(piece_count, gate_count, up_depth, width, *refs):
    pieces, refs = refs[:piece_count], refs[piece_count:]
    gates, refs = refs[:gate_count], refs[gate_count:]
    up_hbm, down_hbm, keep_ref, send_ref = refs[:4]
    up_buf, down_buf, x, gate_sum, up_sum, active, up_sem, down_sem = refs[4:]
    ring = up_buf.shape[0]
    down_ring = down_buf.shape[0]
    up_steps = up_hbm.shape[0] // up_depth
    down_steps = down_hbm.shape[1] // width
    half = keep_ref.shape[0]

    def up_rows(step):
        return pl.ds(pl.multiple_of(step * up_depth, up_depth), up_depth)

    def up_copy(step, slot):
        return pltpu.make_async_copy(
            up_hbm.at[up_rows(step), :], up_buf.at[slot], up_sem.at[slot]
        )

    def down_copy(step, slot):
        columns = pl.ds(pl.multiple_of(step * width, width), width)
        return pltpu.make_async_copy(
            down_hbm.at[:, columns], down_buf.at[slot], down_sem.at[slot]
        )

    for step in range(min(ring, up_steps)):
        up_copy(step, step).start()
    for step in range(min(down_ring, down_steps)):
        down_copy(step, step).start()
    at = 0
    for piece in pieces:
        x[at : at + piece.shape[0], :] = piece[...]
        at += piece.shape[0]
    gate_sum[...] = jnp.zeros_like(gate_sum)
    up_sum[...] = jnp.zeros_like(up_sum)

    depth = 1024
    offset = 0
    for part in gates:

        @pl.loop(0, part.shape[0] // depth)
        def _(step):
            rows = pl.ds(pl.multiple_of(step * depth, depth), depth)
            columns = pl.ds(pl.multiple_of(offset + step * depth, depth), depth)
            gate_sum[...] += jnp.dot(
                x[:, columns], part[rows, :], preferred_element_type=jnp.float32
            )

        offset += part.shape[0]

    @pl.loop(0, up_steps)
    def _(step):
        slot = lax.rem(step, ring)
        up_copy(step, slot).wait()
        up_sum[...] += jnp.dot(
            x[:, up_rows(step)], up_buf[slot], preferred_element_type=jnp.float32
        )

        @pl.when(step + ring < up_steps)
        def _():
            up_copy(step + ring, slot).start()

    gate_proj = gate_sum[...]
    active[...] = (gate_proj / (1.0 + jnp.exp(-gate_proj)) * up_sum[...]).astype(jnp.bfloat16)

    @pl.loop(0, down_steps)
    def _(step):
        slot = lax.rem(step, down_ring)
        columns = pl.ds(pl.multiple_of(step * width, width), width)
        down_copy(step, slot).wait()
        out = jnp.dot(active[...], down_buf[slot], preferred_element_type=jnp.float32)
        keep_ref[:, columns] = out[:half]
        send_ref[:, columns] = out[half:].astype(jnp.bfloat16)

        @pl.when(step + down_ring < down_steps)
        def _():
            down_copy(step + down_ring, slot).start()


def expert_ffn(pieces, gates, w_up, w_down):
    rows = sum(piece.shape[0] for piece in pieces)
    model_width, units = w_up.shape
    up_depth, ring = 512, 4
    width, down_ring = 512, 6
    return pl.pallas_call(
        functools.partial(ffn_kernel, len(pieces), len(gates), up_depth, width),
        out_shape=(
            jax.ShapeDtypeStruct((rows // 2, model_width), jnp.float32),
            jax.ShapeDtypeStruct((rows // 2, model_width), jnp.bfloat16),
        ),
        in_specs=[VMEM] * (len(pieces) + len(gates)) + [HBM, HBM],
        out_specs=(VMEM, VMEM),
        scratch_shapes=[
            pltpu.VMEM((ring, up_depth, units), jnp.bfloat16),
            pltpu.VMEM((down_ring, units, width), jnp.bfloat16),
            pltpu.VMEM((rows, model_width), jnp.bfloat16),
            pltpu.VMEM((rows, units), jnp.float32),
            pltpu.VMEM((rows, units), jnp.float32),
            pltpu.VMEM((rows, units), jnp.bfloat16),
            pltpu.SemaphoreType.DMA((ring,)),
            pltpu.SemaphoreType.DMA((down_ring,)),
        ],
        compiler_params=pltpu.CompilerParams(vmem_limit_bytes=24 * MIB),
        cost_estimate=pl.CostEstimate(
            flops=6 * rows * model_width * units,
            bytes_accessed=6 * model_width * units,
            transcendentals=rows * units,
        ),
    )(*pieces, *gates, w_up, w_down)


def split_kernel(keep_ref, received_ref, *refs):
    kept_ref, sent_refs = refs[-1], refs[-2]
    total = keep_ref[...] + received_ref[...].astype(jnp.float32)
    at = kept_ref.shape[0]
    kept_ref[...] = total[:at]
    sent_refs[...] = total[at:].astype(jnp.bfloat16)


def split_in_two(keep, received):
    half, width = keep.shape[0] // 2, keep.shape[1]
    sent, kept = pl.pallas_call(
        split_kernel,
        in_specs=[VMEM, VMEM],
        out_specs=(VMEM, VMEM),
        out_shape=(
            jax.ShapeDtypeStruct((half, width), jnp.bfloat16),
            jax.ShapeDtypeStruct((half, width), jnp.float32),
        ),
        compiler_params=pltpu.CompilerParams(vmem_limit_bytes=16 * MIB),
    )(keep, received)
    return kept, sent


def split_by_expert_kernel(keep_ref, received_ref, after, kept_ref, *sent_refs):
    total = keep_ref[...] + received_ref[...].astype(jnp.float32)
    rows = kept_ref.shape[0]
    kept_ref[...] = total[:rows]
    for k, sent_ref in enumerate(sent_refs):
        sent_ref[...] = total[(k + 1) * rows : (k + 2) * rows].astype(jnp.bfloat16)


def split_by_expert(keep, received, after):
    rows, width = keep.shape[0] // EXPERTS, keep.shape[1]
    return pl.pallas_call(
        split_by_expert_kernel,
        in_specs=[VMEM, VMEM, HBM],
        out_specs=(VMEM,) * EXPERTS,
        out_shape=(jax.ShapeDtypeStruct((rows, width), jnp.float32),)
        + (jax.ShapeDtypeStruct((rows, width), jnp.bfloat16),) * (EXPERTS - 1),
        compiler_params=pltpu.CompilerParams(vmem_limit_bytes=16 * MIB),
    )(keep, received, after)


def finish_kernel(hidden_ref, coefficient_ref, kept_ref, *refs):
    received_refs, out_ref = refs[:-1], refs[-1]
    mixture = coefficient_ref[:, 0:1] * kept_ref[...]
    for k, received_ref in enumerate(received_refs):
        mixture += coefficient_ref[:, k + 1 : k + 2] * received_ref[...].astype(jnp.float32)
    out_ref[...] = (hidden_ref[...].astype(jnp.float32) + mixture).astype(jnp.bfloat16)


def finish(hidden, coefficient, kept, received):
    return pl.pallas_call(
        finish_kernel,
        in_specs=[VMEM] * (3 + len(received)),
        out_specs=VMEM,
        out_shape=jax.ShapeDtypeStruct(hidden.shape, jnp.bfloat16),
        compiler_params=pltpu.CompilerParams(vmem_limit_bytes=8 * MIB),
    )(hidden, coefficient, kept, *received)


def attend_kernel(
    lengths_ref, queries_ref, keys_ref, values_ref, context_ref, query_heads, context_heads
):
    row_count, cache_span, width = keys_ref.shape
    group = HEADS // KV_HEADS
    for h in range(HEADS):
        query_heads[:, h, :] = queries_ref[:, h * HEAD_DIM : (h + 1) * HEAD_DIM].astype(jnp.float32)
    own_head = lax.broadcasted_iota(jnp.int32, (HEADS, width), 0) // group
    lane_head = lax.broadcasted_iota(jnp.int32, (HEADS, width), 1) // HEAD_DIM
    on_diagonal = own_head == lane_head
    slot = lax.broadcasted_iota(jnp.int32, (HEADS, cache_span), 1)
    for r in range(row_count):
        spread = jnp.where(on_diagonal, jnp.concatenate([query_heads[r]] * KV_HEADS, axis=1), 0.0)
        scores = lax.dot_general(
            spread.astype(jnp.bfloat16), keys_ref[r], (((1,), (1,)), ((), ())),
            preferred_element_type=jnp.float32,
        ) * HEAD_DIM ** (-0.5)
        scores = jnp.where(slot < lengths_ref[r], scores, -jnp.inf)
        raised = jnp.exp(scores - jnp.max(scores, axis=-1, keepdims=True))
        weights = (raised / jnp.sum(raised, axis=-1, keepdims=True)).astype(jnp.bfloat16)
        mixed = jnp.dot(weights, values_ref[r], preferred_element_type=jnp.float32)
        mixed = jnp.where(on_diagonal, mixed, 0.0)
        folded = mixed[:, :HEAD_DIM]
        for j in range(1, KV_HEADS):
            folded = folded + mixed[:, j * HEAD_DIM : (j + 1) * HEAD_DIM]
        context_heads[r] = folded
    for h in range(HEADS):
        context_ref[:, h * HEAD_DIM : (h + 1) * HEAD_DIM] = context_heads[:, h, :].astype(jnp.bfloat16)


def attend(queries, keys_cache, values_cache, lengths):
    row_count, cache_span, width = keys_cache.shape
    vmem = pl.BlockSpec(memory_space=pltpu.VMEM)
    return pl.pallas_call(
        attend_kernel,
        out_shape=jax.ShapeDtypeStruct(queries.shape, jnp.bfloat16),
        in_specs=[pl.BlockSpec(memory_space=pltpu.SMEM), vmem, vmem, vmem],
        out_specs=vmem,
        scratch_shapes=[
            pltpu.VMEM((row_count, HEADS, HEAD_DIM), jnp.float32),
            pltpu.VMEM((row_count, HEADS, HEAD_DIM), jnp.float32),
        ],
        compiler_params=pltpu.CompilerParams(vmem_limit_bytes=8 * MIB),
        cost_estimate=pl.CostEstimate(
            flops=4 * row_count * HEADS * cache_span * width,
            bytes_accessed=4 * row_count * cache_span * width,
            transcendentals=row_count * HEADS * cache_span,
        ),
    )(lengths, queries, keys_cache, values_cache)


def local(
    queries,
    keys_cache,
    values_cache,
    lengths,
    hidden,
    norm_gain,
    expert_ids,
    gate_weights,
    w_gate,
    w_up,
    w_down,
):
    devices = lax.axis_size("pool")
    group_size = devices // EXPERTS
    own_rows = hidden.shape[0]

    def swap(value, distance):
        return lax.ppermute(value, "pool", [(i, i ^ distance) for i in range(devices)])

    near = []
    distance = 1
    while distance < group_size:
        near.append(distance)
        distance *= 2

    depth = w_gate.shape[0]
    normed = normalize(hidden, norm_gain)
    (gate_low,) = prefetch([(w_gate, 0, depth // 2)], normed, 36)
    blocks = [normed] + [swap(normed, k * group_size) for k in range(1, EXPERTS)]
    x = merge(blocks, [gate_low])
    (gate_high,) = prefetch([(w_gate, depth // 2, depth // 2)], x, 36)
    pieces, after = [x], [gate_high]
    for distance in reversed(near):
        arrived = [swap(piece, distance) for piece in pieces]
        if after:
            arrived[0] = merge(arrived[:1], after)
        pieces, after = pieces + arrived, []
    keep, send = expert_ffn(pieces, (gate_low, gate_high), w_up, w_down)

    context = attend(queries, keys_cache, values_cache, lengths)
    own_expert = lax.axis_index("pool") // group_size
    order = own_expert ^ jnp.arange(EXPERTS, dtype=jnp.int32)
    named = expert_ids[:, :, None] == order[None, None, :]
    coefficient = jnp.sum(
        jnp.where(named, gate_weights.astype(jnp.float32)[:, :, None], 0.0), axis=1
    )
    for distance in near[:-1]:
        keep, send = split_in_two(keep, swap(send, distance))
    kept, *sent = split_by_expert(keep, swap(send, near[-1]), context)
    received = [swap(block, (k + 1) * group_size) for k, block in enumerate(sent)]
    moe_out = finish(hidden, coefficient, kept, received)
    return (context, moe_out)


def solution(mesh):
    return jax.shard_map(
        local,
        mesh=mesh,
        in_specs=(
            P(("groups", "pool"), None),
            P(("groups", "pool"), None, None),
            P(("groups", "pool"), None, None),
            P(("groups", "pool")),
            P(("groups", "pool"), None),
            P(),
            P(("groups", "pool"), None),
            P(("groups", "pool"), None),
            P(None, "pool"),
            P(None, "pool"),
            P("pool", None),
        ),
        out_specs=(P(("groups", "pool"), None), P(("groups", "pool"), None)),
        check_vma=False,
    )
```

time: 66.6 us -> 60 us (0.901)
  waiting for transfers between devices: 16.2 us -> 8.03 us
  Pallas kernels: 26.8 us -> 34 us
  matrix products: 2.88 us -> 0 us
  other arithmetic: 1.98 us -> 0.09 us
  local copies, waits for them, and re-layouts: 3.85 us -> 3.11 us
    ppermute x10 -> x11, waiting for transfers between devices: 16.2 us -> 8.03 us  [swap(): lax.ppermute(value, 'pool', [(i, i ^ distance) for i in range(devices)])]
    pallas_call x1 -> x9, Pallas kernels: 26.7 us -> 32.4 us  [the longest x1 18.6 us: expert_ffn(): pl.pallas_call(functools.partial(ffn_kernel, len(pieces), len(gates), up_...]
    dot_general x2 -> x0, matrix products: 2.88 us -> none  [the longest x1 1.98 us: attend(): jnp.einsum('rkgl,rlkd->rkgd', attn_weights, value_heads, preferred_elemen...]
    unnamed x10 -> x20, local copies, waits for them, and re-layouts: 0.82 us -> 3.11 us
    reshape x2 -> x0, local copies, waits for them, and re-layouts: 1.7 us -> none  [the longest x1 0.86 us: attend(): queries.reshape(row_count, KV_HEADS, HEADS // KV_HEADS, HEAD_DIM)]
    pallas_call x1, Pallas kernels: 0.16 us -> 1.62 us  [normalize(): pl.pallas_call(norm_kernel, out_shape=jax.ShapeDtypeStruct(hidden.shape,...]
    convert_element_type x1, other arithmetic: 0.77 us -> 0.01 us  [local(): gate_weights.astype(jnp.float32)[:, :, None]]
    lt x1 -> x0, other arithmetic: 0.73 us -> none  [attend(): jnp.arange(cache_span, dtype=jnp.int32)[None, None, None, :]]
  transfers between devices with their start and end apart: 10 -> 11, of which waited for: 8 -> 8; matrix products, arithmetic and copies ran while one was open for 8% -> 0% of each run, Pallas kernels for 0% -> 21%
where the time goes in v2:
time: 60 us; the launch traced here: 59.7 us
  Pallas kernels  34 us (57%)
  starting transfers between devices  13.7 us (23%)
  waiting for transfers between devices  8.03 us (13%)
  local copies, waits for them, and re-layouts  3.11 us (5%)
  between operations  0.79 us (1%)
    pallas_call x1, Pallas kernels, expert_ffn(): pl.pallas_call(functools.partial(ffn_kernel, len(pieces), len(gates), up_...  18.6 us
    ppermute x11, starting transfers between devices, swap(): lax.ppermute(value, 'pool', [(i, i ^ distance) for i in range(devices)])  13.7 us
    pallas_call x2, Pallas kernels, prefetch(): pl.pallas_call(functools.partial(prefetch_kernel, tuple((first for _, fir...  9.17 us
    ppermute x11, waiting for transfers between devices, swap(): lax.ppermute(value, 'pool', [(i, i ^ distance) for i in range(devices)])  8.03 us
    pallas_call x1, Pallas kernels, attend(): pl.pallas_call(attend_kernel, out_shape=jax.ShapeDtypeStruct(queries.shap...  3.61 us
    unnamed x20, local copies, waits for them, and re-layouts  3.11 us
    pallas_call x1, Pallas kernels, normalize(): pl.pallas_call(norm_kernel, out_shape=jax.ShapeDtypeStruct(hidden.shape,...  1.62 us
  transfers between devices with their start and end apart: 11, of which 8 were waited for; matrix products, arithmetic and copies ran while one was open for 0% of the time, Pallas kernels for 21%

profile of v2, /device:TPU:0, one launch (start us, length us, event | category | flops | bytes accessed | tf_op | source)
XLA Modules:
  0.0 59.7 jit_solution(14840978721125617841)
XLA Ops:
  0.6 1.6 %shard_map.123.refs_1_.refs_0_ = bf16[4,6144]{1,0:T(4,128)(2,1)} custom-call(bf16[4,6144]{1,0:T(4,128)(2,1)} %hidden_ref.1, bf16[6144]{0:T(1024)(128)(2,1)} %gain_hbm.1), custom_call_target="tpu_custom_call" | custom-call | tf_op jit(solution)/shard_map/pallas_call | solution.py:35
  2.3 3.1 %collective-permute-start = (bf16[4,6144]{1,0:T(4,128)(2,1)}, bf16[4,6144]{1,0:T(4,128)(2,1)S(1)}, u32[]{:S(2)}, u32[]{:S(2)}) collective-permute-start(bf16[4,6144]{1,0:T(4,128)(2,1)} %shard_map.123.refs_1_.refs_0_), channel_id=1, source_target_pairs={{0,4},{1,5},{2,6},{3,7},{4,0},{5,1},{6,2},{7,3},{8,12},{9,13},{10,... | collective-permute-start | bytes 147464 | tf_op jit(solution)/shard_map/ppermute | solution.py:334
  5.3 2.6 %collective-permute-start.1 = (bf16[4,6144]{1,0:T(4,128)(2,1)}, bf16[4,6144]{1,0:T(4,128)(2,1)S(1)}, u32[]{:S(2)}, u32[]{:S(2)}) collective-permute-start(bf16[4,6144]{1,0:T(4,128)(2,1)} %shard_map.123.refs_1_.refs_0_), channel_id=1, source_target_pairs={{0,8},{1,9},{2,10},{3,11},{4,12},{5,13},{6,14},{7,15},{8,0},{9,1},... | collective-permute-start | bytes 147464 | tf_op jit(solution)/shard_map/ppermute | solution.py:334
  7.9 0.0 collective-permute-start.2
  7.9 0.0 copy-start.2
  7.9 0.9 %copy-done.2 = bf16[4,6144]{1,0:T(4,128)(2,1)S(1)} copy-done((bf16[4,6144]{1,0:T(4,128)(2,1)S(1)}, bf16[4,6144]{1,0:T(4,128)(2,1)}, u32[]{:S(2)}) %copy-start.2) | copy-done | bytes 49176
  8.8 0.0 copy-start.3
  8.8 4.6 %shard_map.124.refs_4_ = bf16[3072,2048]{1,0:T(8,128)(2,1)S(1)} custom-call(bf16[6144,2048]{1,0:T(8,128)(2,1)} %refs_0_.3, bf16[4,6144]{1,0:T(4,128)(2,1)S(1)} %copy-done.2), custom_call_target="tpu_custom_call" | custom-call | bytes 12582912 | tf_op jit(solution)/shard_map/pallas_call | solution.py:80
  13.4 0.0 collective-permute-done.refs_1_
  13.4 0.0 collective-permute-done.1.refs_2_
  13.4 0.6 %collective-permute-done.2.refs_3_ = bf16[4,6144]{1,0:T(4,128)(2,1)S(1)} collective-permute-done((bf16[4,6144]{1,0:T(4,128)(2,1)}, bf16[4,6144]{1,0:T(4,128)(2,1)S(1)}, u32[]{:S(2)}, u32[]{:S(2)}) %collective-permute-start.2) | collective-permute-done | bytes 49184 | tf_op jit(solution)/shard_map/ppermute | solution.py:334
  14.0 0.0 copy-done.3
  14.0 0.1 shard_map.125.refs_1_.refs_0_
  14.1 1.6 %collective-permute-start.3 = (bf16[16,6144]{1,0:T(8,128)(2,1)S(1)}, bf16[16,6144]{1,0:T(8,128)(2,1)S(1)}, u32[]{:S(2)}, u32[]{:S(2)}) collective-permute-start(bf16[16,6144]{1,0:T(8,128)(2,1)S(1)} %shard_map.125.refs_1_.refs_0_), channel_id=1, source_target_pairs={{0,2},{1,3},{2,0},{3,1},{4,6},{5,7},{6,4},{7,5},{8,10},{9,11},{10,... | collective-permute-start | bytes 589832 | tf_op jit(solution)/shard_map/ppermute | solution.py:334
  15.7 4.6 %shard_map.126.refs_1_.refs_5_ = bf16[3072,2048]{1,0:T(8,128)(2,1)S(1)} custom-call(bf16[6144,2048]{1,0:T(8,128)(2,1)} %refs_0_.3, bf16[16,6144]{1,0:T(8,128)(2,1)S(1)} %shard_map.125.refs_1_.refs_0_), custom_call_target="tpu_custom_call" | custom-call | bytes 12582912 | tf_op jit(solution)/shard_map/pallas_call | solution.py:80
  20.3 0.1 collective-permute-start.4
  20.3 0.0 collective-permute-done.3.refs_0_
  20.4 0.0 copy-start.9
  20.4 0.0 copy-start
  20.4 0.0 copy-start.6
  20.4 0.0 copy-start.7
  20.4 0.0 copy-start.8
  20.4 0.0 copy-start.4
  20.4 0.5 collective-permute-start.5
  21.0 0.8 %collective-permute-done.4.refs_2_ = bf16[16,6144]{1,0:T(8,128)(2,1)S(1)} collective-permute-done((bf16[16,6144]{1,0:T(8,128)(2,1)S(1)}, bf16[16,6144]{1,0:T(8,128)(2,1)S(1)}, u32[]{:S(2)}, u32[]{:S(2)}) %collective-permute-start.4) | collective-permute-done | bytes 196640 | tf_op jit(solution)/shard_map/ppermute | solution.py:334
  21.8 0.3 collective-permute-done.5.refs_3_
  22.1 18.6 %shard_map.128 = (f32[32,6144]{1,0:T(8,128)S(1)}, bf16[32,6144]{1,0:T(8,128)(2,1)S(1)}) custom-call(bf16[16,6144]{1,0:T(8,128)(2,1)S(1)} %shard_map.125.refs_1_.refs_0_, bf16[16,6144]{1,0:T(8,128)(2,1)S(1)} %shard_map.127.refs_1_, bf16[16,6144]{1,0:T(8,128)(2,1)S(1)} %collective-permute-done.4.refs_2_, bf16[16,6144]{1,0:T(8,128)(2,1)S(1)} %collective-permute-done.5.refs_3_, ...), custom_call_target="tpu_custom_call" | custom-call | flops 4831838208 | bytes 75497472 | tf_op jit(solution)/shard_map/pallas_call | solution.py:177
  40.7 0.4 collective-permute-start.6
  41.1 1.4 %collective-permute-done.6.received_ref = bf16[32,6144]{1,0:T(8,128)(2,1)S(1)} collective-permute-done((bf16[32,6144]{1,0:T(8,128)(2,1)S(1)}, bf16[32,6144]{1,0:T(8,128)(2,1)S(1)}, u32[]{:S(2)}, u32[]{:S(2)}) %collective-permute-start.6) | collective-permute-done | bytes 393248 | tf_op jit(solution)/shard_map/ppermute | solution.py:334
  42.5 0.1 shard_map.129
  42.5 0.9 %collective-permute-start.7 = (bf16[16,6144]{1,0:T(8,128)(2,1)S(1)}, bf16[16,6144]{1,0:T(8,128)(2,1)S(1)}, u32[]{:S(2)}, u32[]{:S(2)}) collective-permute-start(bf16[16,6144]{1,0:T(8,128)(2,1)S(1)} %get-tuple-element.13), channel_id=1, source_target_pairs={{0,2},{1,3},{2,0},{3,1},{4,6},{5,7},{6,4},{7,5},{8,10},{9,11},{10,... | collective-permute-start | bytes 589832 | tf_op jit(solution)/shard_map/ppermute | solution.py:334
  43.5 0.0 copy-done.9
  43.5 0.0 copy-done
  43.5 0.0 copy-done.6
  43.5 0.0 copy-done.7
  43.5 0.0 copy-start.1
  43.5 1.4 %copy-done.1 = bf16[4,192,1024]{2,1,0:T(8,128)(2,1)S(1)} copy-done((bf16[4,192,1024]{2,1,0:T(8,128)(2,1)S(1)}, bf16[4,192,1024]{2,1,0:T(8,128)(2,1)}, u32[]{:S(2)}) %copy-start.1) | copy-done | bytes 1572888
  44.9 3.6 %shard_map.122.after = bf16[4,6144]{1,0:T(4,128)(2,1)} custom-call(s32[4]{0:T(128)S(1)} %copy-done.7, bf16[4,6144]{1,0:T(4,128)(2,1)S(1)} %copy-done.6, bf16[4,192,1024]{2,1,0:T(8,128)(2,1)S(1)} %copy-done, bf16[4,192,1024]{2,1,0:T(8,128)(2,1)S(1)} %copy-done.1), custom_call_target="tpu_custom_call" | custom-call | flops 150994944 | bytes 3145728 | tf_op jit(solution)/shard_map/pallas_call | solution.py:298
  48.5 1.3 %collective-permute-done.7.received_ref = bf16[16,6144]{1,0:T(8,128)(2,1)S(1)} collective-permute-done((bf16[16,6144]{1,0:T(8,128)(2,1)S(1)}, bf16[16,6144]{1,0:T(8,128)(2,1)S(1)}, u32[]{:S(2)}, u32[]{:S(2)}) %collective-permute-start.7) | collective-permute-done | bytes 196640 | tf_op jit(solution)/shard_map/ppermute | solution.py:334
  49.8 0.0 copy-start.5
  49.8 0.8 %copy-done.5 = bf16[4,6144]{1,0:T(4,128)(2,1)S(1)} copy-done((bf16[4,6144]{1,0:T(4,128)(2,1)S(1)}, bf16[4,6144]{1,0:T(4,128)(2,1)}, u32[]{:S(2)}) %copy-start.5) | copy-done | bytes 49176
  50.6 0.1 shard_map.130
  50.6 3.3 %collective-permute-start.10 = (bf16[4,6144]{1,0:T(4,128)(2,1)S(1)}, bf16[4,6144]{1,0:T(4,128)(2,1)S(1)}, u32[]{:S(2)}, u32[]{:S(2)}) collective-permute-start(bf16[4,6144]{1,0:T(4,128)(2,1)S(1)} %get-tuple-element.17), channel_id=1, source_target_pairs={{0,12},{1,13},{2,14},{3,15},{4,8},{5,9},{6,10},{7,11},{8,4},{9,5},... | collective-permute-start | bytes 147464 | tf_op jit(solution)/shard_map/ppermute | solution.py:334
  53.9 0.0 collective-permute-start.8
  53.9 1.2 %collective-permute-start.9 = (bf16[4,6144]{1,0:T(4,128)(2,1)S(1)}, bf16[4,6144]{1,0:T(4,128)(2,1)S(1)}, u32[]{:S(2)}, u32[]{:S(2)}) collective-permute-start(bf16[4,6144]{1,0:T(4,128)(2,1)S(1)} %get-tuple-element.16), channel_id=1, source_target_pairs={{0,8},{1,9},{2,10},{3,11},{4,12},{5,13},{6,14},{7,15},{8,0},{9,1},... | collective-permute-start | bytes 147464 | tf_op jit(solution)/shard_map/ppermute | solution.py:334
  55.1 0.0 copy-done.8
  55.1 0.1 select_reduce_fusion.coefficient_ref
  55.2 1.5 %collective-permute-done.10.refs_2_ = bf16[4,6144]{1,0:T(4,128)(2,1)S(1)} collective-permute-done((bf16[4,6144]{1,0:T(4,128)(2,1)S(1)}, bf16[4,6144]{1,0:T(4,128)(2,1)S(1)}, u32[]{:S(2)}, u32[]{:S(2)}) %collective-permute-start.10) | collective-permute-done | bytes 49184 | tf_op jit(solution)/shard_map/ppermute | solution.py:334
  56.7 1.3 %collective-permute-done.8.refs_0_ = bf16[4,6144]{1,0:T(4,128)(2,1)S(1)} collective-permute-done((bf16[4,6144]{1,0:T(4,128)(2,1)S(1)}, bf16[4,6144]{1,0:T(4,128)(2,1)S(1)}, u32[]{:S(2)}, u32[]{:S(2)}) %collective-permute-start.8) | collective-permute-done | bytes 49184 | tf_op jit(solution)/shard_map/ppermute | solution.py:334
  58.0 0.9 %collective-permute-done.9.refs_1_ = bf16[4,6144]{1,0:T(4,128)(2,1)S(1)} collective-permute-done((bf16[4,6144]{1,0:T(4,128)(2,1)S(1)}, bf16[4,6144]{1,0:T(4,128)(2,1)S(1)}, u32[]{:S(2)}, u32[]{:S(2)}) %collective-permute-start.9) | collective-permute-done | bytes 49184 | tf_op jit(solution)/shard_map/ppermute | solution.py:334
  58.9 0.0 copy-done.4
  58.9 0.8 %shard_map.131 = bf16[4,6144]{1,0:T(4,128)(2,1)} custom-call(bf16[4,6144]{1,0:T(4,128)(2,1)S(1)} %copy-done.4, f32[4,4]{1,0:T(4,128)S(1)} %select_reduce_fusion.coefficient_ref, f32[4,6144]{1,0:T(4,128)S(1)} %get-tuple-element.14.kept_ref, bf16[4,6144]{1,0:T(4,128)(2,1)S(1)} %collective-permute-done.8.refs_0_, ...), custom_call_target="tpu_custom_call" | custom-call | tf_op jit(solution)/shard_map/pallas_call | solution.py:256
  (3 shorter events, 0.0 us)
Async XLA Ops:
  2.3 11.2 %collective-permute-start = (bf16[4,6144]{1,0:T(4,128)(2,1)}, bf16[4,6144]{1,0:T(4,128)(2,1)S(1)}, u32[]{:S(2)}, u32[]{:S(2)}) collective-permute-start(bf16[4,6144]{1,0:T(4,128)(2,1)} %shard_map.123.refs_1_.refs_0_), channel_id=1, source_target_pairs={{0,4},{1,5},{2,6},{3,7},{4,0},{5,1},{6,2},{7,3},{8,12},{9,13},{10,... | collective-permute-start | bytes 147464 | tf_op jit(solution)/shard_map/ppermute | solution.py:334
  5.3 8.1 %collective-permute-start.1 = (bf16[4,6144]{1,0:T(4,128)(2,1)}, bf16[4,6144]{1,0:T(4,128)(2,1)S(1)}, u32[]{:S(2)}, u32[]{:S(2)}) collective-permute-start(bf16[4,6144]{1,0:T(4,128)(2,1)} %shard_map.123.refs_1_.refs_0_), channel_id=1, source_target_pairs={{0,8},{1,9},{2,10},{3,11},{4,12},{5,13},{6,14},{7,15},{8,0},{9,1},... | collective-permute-start | bytes 147464 | tf_op jit(solution)/shard_map/ppermute | solution.py:334
  7.9 6.1 %collective-permute-start.2 = (bf16[4,6144]{1,0:T(4,128)(2,1)}, bf16[4,6144]{1,0:T(4,128)(2,1)S(1)}, u32[]{:S(2)}, u32[]{:S(2)}) collective-permute-start(bf16[4,6144]{1,0:T(4,128)(2,1)} %shard_map.123.refs_1_.refs_0_), channel_id=1, source_target_pairs={{0,12},{1,13},{2,14},{3,15},{4,8},{5,9},{6,10},{7,11},{8,4},{9,5},... | collective-permute-start | bytes 147464 | tf_op jit(solution)/shard_map/ppermute | solution.py:334
  7.9 0.9 %copy-start.2 = (bf16[4,6144]{1,0:T(4,128)(2,1)S(1)}, bf16[4,6144]{1,0:T(4,128)(2,1)}, u32[]{:S(2)}) copy-start(bf16[4,6144]{1,0:T(4,128)(2,1)} %shard_map.123.refs_1_.refs_0_) | copy-start | bytes 147460
  8.8 5.2 %copy-start.3 = (bf16[4,6144]{1,0:T(4,128)(2,1)S(1)}, bf16[4,6144]{1,0:T(4,128)(2,1)}, u32[]{:S(2)}) copy-start(bf16[4,6144]{1,0:T(4,128)(2,1)} %shard_map.123.refs_1_.refs_0_) | copy-start | bytes 147460
  14.1 6.2 %collective-permute-start.3 = (bf16[16,6144]{1,0:T(8,128)(2,1)S(1)}, bf16[16,6144]{1,0:T(8,128)(2,1)S(1)}, u32[]{:S(2)}, u32[]{:S(2)}) collective-permute-start(bf16[16,6144]{1,0:T(8,128)(2,1)S(1)} %shard_map.125.refs_1_.refs_0_), channel_id=1, source_target_pairs={{0,2},{1,3},{2,0},{3,1},{4,6},{5,7},{6,4},{7,5},{8,10},{9,11},{10,... | collective-permute-start | bytes 589832 | tf_op jit(solution)/shard_map/ppermute | solution.py:334
  20.3 1.5 %collective-permute-start.4 = (bf16[16,6144]{1,0:T(8,128)(2,1)S(1)}, bf16[16,6144]{1,0:T(8,128)(2,1)S(1)}, u32[]{:S(2)}, u32[]{:S(2)}) collective-permute-start(bf16[16,6144]{1,0:T(8,128)(2,1)S(1)} %shard_map.125.refs_1_.refs_0_), channel_id=1, source_target_pairs={{0,1},{1,0},{2,3},{3,2},{4,5},{5,4},{6,7},{7,6},{8,9},{9,8},{10,11... | collective-permute-start | bytes 589832 | tf_op jit(solution)/shard_map/ppermute | solution.py:334
  20.4 23.1 %copy-start.9 = (bf16[4,2]{0,1:T(2,128)(2,1)S(1)}, bf16[4,2]{0,1:T(2,128)(2,1)}, u32[]{:S(2)}) copy-start(bf16[4,2]{0,1:T(2,128)(2,1)} %param.18) | copy-start | bytes 52
  20.4 23.1 %copy-start = (bf16[4,192,1024]{2,1,0:T(8,128)(2,1)S(1)}, bf16[4,192,1024]{2,1,0:T(8,128)(2,1)}, u32[]{:S(2)}) copy-start(bf16[4,192,1024]{2,1,0:T(8,128)(2,1)} %keys_ref.1) | copy-start | bytes 4718596
  20.4 23.1 %copy-start.6 = (bf16[4,6144]{1,0:T(4,128)(2,1)S(1)}, bf16[4,6144]{1,0:T(4,128)(2,1)}, u32[]{:S(2)}) copy-start(bf16[4,6144]{1,0:T(4,128)(2,1)} %queries_ref.1) | copy-start | bytes 147460
  20.4 23.1 %copy-start.7 = (s32[4]{0:T(128)S(1)}, s32[4]{0:T(128)}, u32[]{:S(2)}) copy-start(s32[4]{0:T(128)} %lengths_ref.1) | copy-start | bytes 52
  20.4 34.7 %copy-start.8 = (s32[4,2]{0,1:T(2,128)S(1)}, s32[4,2]{0,1:T(2,128)}, u32[]{:S(2)}) copy-start(s32[4,2]{0,1:T(2,128)} %param.17) | copy-start | bytes 100
  20.4 38.5 %copy-start.4 = (bf16[4,6144]{1,0:T(4,128)(2,1)S(1)}, bf16[4,6144]{1,0:T(4,128)(2,1)}, u32[]{:S(2)}) copy-start(bf16[4,6144]{1,0:T(4,128)(2,1)} %hidden_ref.1) | copy-start | bytes 147460
  20.4 1.6 %collective-permute-start.5 = (bf16[16,6144]{1,0:T(8,128)(2,1)S(1)}, bf16[16,6144]{1,0:T(8,128)(2,1)S(1)}, u32[]{:S(2)}, u32[]{:S(2)}) collective-permute-start(bf16[16,6144]{1,0:T(8,128)(2,1)S(1)} %shard_map.127.refs_1_), channel_id=1, source_target_pairs={{0,1},{1,0},{2,3},{3,2},{4,5},{5,4},{6,7},{7,6},{8,9},{9,8},{10,11... | collective-permute-start | bytes 589832 | tf_op jit(solution)/shard_map/ppermute | solution.py:334
  40.7 1.8 %collective-permute-start.6 = (bf16[32,6144]{1,0:T(8,128)(2,1)S(1)}, bf16[32,6144]{1,0:T(8,128)(2,1)S(1)}, u32[]{:S(2)}, u32[]{:S(2)}) collective-permute-start(bf16[32,6144]{1,0:T(8,128)(2,1)S(1)} %get-tuple-element.11), channel_id=1, source_target_pairs={{0,1},{1,0},{2,3},{3,2},{4,5},{5,4},{6,7},{7,6},{8,9},{9,8},{10,11... | collective-permute-start | bytes 1179656 | tf_op jit(solution)/shard_map/ppermute | solution.py:334
  42.5 7.2 %collective-permute-start.7 = (bf16[16,6144]{1,0:T(8,128)(2,1)S(1)}, bf16[16,6144]{1,0:T(8,128)(2,1)S(1)}, u32[]{:S(2)}, u32[]{:S(2)}) collective-permute-start(bf16[16,6144]{1,0:T(8,128)(2,1)S(1)} %get-tuple-element.13), channel_id=1, source_target_pairs={{0,2},{1,3},{2,0},{3,1},{4,6},{5,7},{6,4},{7,5},{8,10},{9,11},{10,... | collective-permute-start | bytes 589832 | tf_op jit(solution)/shard_map/ppermute | solution.py:334
  43.5 1.4 %copy-start.1 = (bf16[4,192,1024]{2,1,0:T(8,128)(2,1)S(1)}, bf16[4,192,1024]{2,1,0:T(8,128)(2,1)}, u32[]{:S(2)}) copy-start(bf16[4,192,1024]{2,1,0:T(8,128)(2,1)} %values_ref.1) | copy-start | bytes 4718596
  49.8 0.8 %copy-start.5 = (bf16[4,6144]{1,0:T(4,128)(2,1)S(1)}, bf16[4,6144]{1,0:T(4,128)(2,1)}, u32[]{:S(2)}) copy-start(bf16[4,6144]{1,0:T(4,128)(2,1)} %shard_map.122.after) | copy-start | bytes 147460
  50.6 6.1 %collective-permute-start.10 = (bf16[4,6144]{1,0:T(4,128)(2,1)S(1)}, bf16[4,6144]{1,0:T(4,128)(2,1)S(1)}, u32[]{:S(2)}, u32[]{:S(2)}) collective-permute-start(bf16[4,6144]{1,0:T(4,128)(2,1)S(1)} %get-tuple-element.17), channel_id=1, source_target_pairs={{0,12},{1,13},{2,14},{3,15},{4,8},{5,9},{6,10},{7,11},{8,4},{9,5},... | collective-permute-start | bytes 147464 | tf_op jit(solution)/shard_map/ppermute | solution.py:334
  53.9 4.1 %collective-permute-start.8 = (bf16[4,6144]{1,0:T(4,128)(2,1)S(1)}, bf16[4,6144]{1,0:T(4,128)(2,1)S(1)}, u32[]{:S(2)}, u32[]{:S(2)}) collective-permute-start(bf16[4,6144]{1,0:T(4,128)(2,1)S(1)} %get-tuple-element.15), channel_id=1, source_target_pairs={{0,4},{1,5},{2,6},{3,7},{4,0},{5,1},{6,2},{7,3},{8,12},{9,13},{10,... | collective-permute-start | bytes 147464 | tf_op jit(solution)/shard_map/ppermute | solution.py:334
  53.9 5.0 %collective-permute-start.9 = (bf16[4,6144]{1,0:T(4,128)(2,1)S(1)}, bf16[4,6144]{1,0:T(4,128)(2,1)S(1)}, u32[]{:S(2)}, u32[]{:S(2)}) collective-permute-start(bf16[4,6144]{1,0:T(4,128)(2,1)S(1)} %get-tuple-element.16), channel_id=1, source_target_pairs={{0,8},{1,9},{2,10},{3,11},{4,12},{5,13},{6,14},{7,15},{8,0},{9,1},... | collective-permute-start | bytes 147464 | tf_op jit(solution)/shard_map/ppermute | solution.py:334

commit v3 on v2

--- a/solution.py
+++ b/solution.py
@@ -90,35 +90,44 @@
     )(*[weights for weights, _, _ in parts], after)
 
 
-def ffn_kernel(piece_count, gate_count, up_depth, width, *refs):
+def ffn_kernel(piece_count, gate_count, *refs):
     pieces, refs = refs[:piece_count], refs[piece_count:]
     gates, refs = refs[:gate_count], refs[gate_count:]
     up_hbm, down_hbm, keep_ref, send_ref = refs[:4]
-    up_buf, down_buf, x, gate_sum, up_sum, active, up_sem, down_sem = refs[4:]
-    ring = up_buf.shape[0]
-    down_ring = down_buf.shape[0]
-    up_steps = up_hbm.shape[0] // up_depth
-    down_steps = down_hbm.shape[1] // width
+    chunks, x, gate_sum, up_sum, active, sems = refs[4:]
+    ring, depth, width = chunks.shape
+    up_steps = up_hbm.shape[0] // depth
+    down_parts = down_hbm.shape[0] // depth
+    down_steps = down_parts * (down_hbm.shape[1] // width)
     half = keep_ref.shape[0]
 
-    def up_rows(step):
-        return pl.ds(pl.multiple_of(step * up_depth, up_depth), up_depth)
-
-    def up_copy(step, slot):
+    def block(index, size):
+        return pl.ds(pl.multiple_of(index * size, size), size)
+
+    def up_copy(step):
+        slot = lax.rem(step, ring)
         return pltpu.make_async_copy(
-            up_hbm.at[up_rows(step), :], up_buf.at[slot], up_sem.at[slot]
+            up_hbm.at[block(step, depth), :], chunks.at[slot], sems.at[slot]
         )
 
-    def down_copy(step, slot):
-        columns = pl.ds(pl.multiple_of(step * width, width), width)
-        return pltpu.make_async_copy(
-            down_hbm.at[:, columns], down_buf.at[slot], down_sem.at[slot]
-        )
-
-    for step in range(min(ring, up_steps)):
-        up_copy(step, step).start()
-    for step in range(min(down_ring, down_steps)):
-        down_copy(step, step).start()
+    def down_copy(step):
+        slot = lax.rem(step + up_steps, ring)
+        part = down_hbm.at[
+            block(lax.rem(step, down_parts), depth), block(lax.div(step, down_parts), width)
+        ]
+        return pltpu.make_async_copy(part, chunks.at[slot], sems.at[slot])
+
+    def issue(step):
+        @pl.when(step < up_steps)
+        def _():
+            up_copy(step).start()
+
+        @pl.when((step >= up_steps) & (step < up_steps + down_steps))
+        def _():
+            down_copy(step - up_steps).start()
+
+    for step in range(ring):
+        issue(jnp.int32(step))
     at = 0
     for piece in pieces:
         x[at : at + piece.shape[0], :] = piece[...]
@@ -126,56 +135,56 @@
     gate_sum[...] = jnp.zeros_like(gate_sum)
     up_sum[...] = jnp.zeros_like(up_sum)
 
-    depth = 1024
+    gate_depth = 1024
     offset = 0
     for part in gates:
 
-        @pl.loop(0, part.shape[0] // depth)
+        @pl.loop(0, part.shape[0] // gate_depth)
         def _(step):
-            rows = pl.ds(pl.multiple_of(step * depth, depth), depth)
-            columns = pl.ds(pl.multiple_of(offset + step * depth, depth), depth)
+            columns = pl.ds(pl.multiple_of(offset + step * gate_depth, gate_depth), gate_depth)
             gate_sum[...] += jnp.dot(
-                x[:, columns], part[rows, :], preferred_element_type=jnp.float32
+                x[:, columns], part[block(step, gate_depth), :], preferred_element_type=jnp.float32
             )
 
         offset += part.shape[0]
 
     @pl.loop(0, up_steps)
     def _(step):
-        slot = lax.rem(step, ring)
-        up_copy(step, slot).wait()
+        up_copy(step).wait()
         up_sum[...] += jnp.dot(
-            x[:, up_rows(step)], up_buf[slot], preferred_element_type=jnp.float32
+            x[:, block(step, depth)], chunks[lax.rem(step, ring)], preferred_element_type=jnp.float32
         )
-
-        @pl.when(step + ring < up_steps)
-        def _():
-            up_copy(step + ring, slot).start()
+        issue(step + ring)
 
     gate_proj = gate_sum[...]
     active[...] = (gate_proj / (1.0 + jnp.exp(-gate_proj)) * up_sum[...]).astype(jnp.bfloat16)
 
-    @pl.loop(0, down_steps)
-    def _(step):
-        slot = lax.rem(step, down_ring)
-        columns = pl.ds(pl.multiple_of(step * width, width), width)
-        down_copy(step, slot).wait()
-        out = jnp.dot(active[...], down_buf[slot], preferred_element_type=jnp.float32)
-        keep_ref[:, columns] = out[:half]
-        send_ref[:, columns] = out[half:].astype(jnp.bfloat16)
-
-        @pl.when(step + down_ring < down_steps)
-        def _():
-            down_copy(step + down_ring, slot).start()
+    @pl.loop(0, down_steps // down_parts)
+    def _(column):
+        for part in range(down_parts):
+            step = column * down_parts + part
+            down_copy(step).wait()
+            out = jnp.dot(
+                active[:, part * depth : (part + 1) * depth],
+                chunks[lax.rem(step + up_steps, ring)],
+                preferred_element_type=jnp.float32,
+            )
+            if part > 0:
+                out += gate_sum[...]
+            if part + 1 < down_parts:
+                gate_sum[...] = out
+            else:
+                keep_ref[:, block(column, width)] = out[:half]
+                send_ref[:, block(column, width)] = out[half:].astype(jnp.bfloat16)
+            issue(step + up_steps + ring)
 
 
 def expert_ffn(pieces, gates, w_up, w_down):
     rows = sum(piece.shape[0] for piece in pieces)
     model_width, units = w_up.shape
-    up_depth, ring = 512, 4
-    width, down_ring = 512, 6
-    return pl.pallas_call(
-        functools.partial(ffn_kernel, len(pieces), len(gates), up_depth, width),
+    ring, depth = 10, min(512, units)
+    return pl.pallas_call(
+        functools.partial(ffn_kernel, len(pieces), len(gates)),
         out_shape=(
             jax.ShapeDtypeStruct((rows // 2, model_width), jnp.float32),
             jax.ShapeDtypeStruct((rows // 2, model_width), jnp.bfloat16),
@@ -183,14 +192,12 @@
         in_specs=[VMEM] * (len(pieces) + len(gates)) + [HBM, HBM],
         out_specs=(VMEM, VMEM),
         scratch_shapes=[
-            pltpu.VMEM((ring, up_depth, units), jnp.bfloat16),
-            pltpu.VMEM((down_ring, units, width), jnp.bfloat16),
+            pltpu.VMEM((ring, depth, units), jnp.bfloat16),
             pltpu.VMEM((rows, model_width), jnp.bfloat16),
             pltpu.VMEM((rows, units), jnp.float32),
             pltpu.VMEM((rows, units), jnp.float32),
             pltpu.VMEM((rows, units), jnp.bfloat16),
             pltpu.SemaphoreType.DMA((ring,)),
-            pltpu.SemaphoreType.DMA((down_ring,)),
         ],
         compiler_params=pltpu.CompilerParams(vmem_limit_bytes=24 * MIB),
         cost_estimate=pl.CostEstimate(
@@ -224,7 +231,7 @@
     return kept, sent
 
 
-def split_by_expert_kernel(keep_ref, received_ref, after, kept_ref, *sent_refs):
+def split_by_expert_kernel(keep_ref, received_ref, token_ref, kept_ref, *sent_refs):
     total = keep_ref[...] + received_ref[...].astype(jnp.float32)
     rows = kept_ref.shape[0]
     kept_ref[...] = total[:rows]
@@ -232,16 +239,16 @@
         sent_ref[...] = total[(k + 1) * rows : (k + 2) * rows].astype(jnp.bfloat16)
 
 
-def split_by_expert(keep, received, after):
+def split_by_expert(keep, received, token):
     rows, width = keep.shape[0] // EXPERTS, keep.shape[1]
     return pl.pallas_call(
         split_by_expert_kernel,
-        in_specs=[VMEM, VMEM, HBM],
+        in_specs=[VMEM, VMEM, VMEM],
         out_specs=(VMEM,) * EXPERTS,
         out_shape=(jax.ShapeDtypeStruct((rows, width), jnp.float32),)
         + (jax.ShapeDtypeStruct((rows, width), jnp.bfloat16),) * (EXPERTS - 1),
         compiler_params=pltpu.CompilerParams(vmem_limit_bytes=16 * MIB),
-    )(keep, received, after)
+    )(keep, received, token)
 
 
 def finish_kernel(hidden_ref, coefficient_ref, kept_ref, *refs):
@@ -263,8 +270,10 @@
 
 
 def attend_kernel(
-    lengths_ref, queries_ref, keys_ref, values_ref, context_ref, query_heads, context_heads
+    lengths_ref, queries_ref, keys_ref, values_ref, context_ref, token_ref,
+    query_heads, context_heads,
 ):
+    token_ref[...] = jnp.zeros_like(token_ref)
     row_count, cache_span, width = keys_ref.shape
     group = HEADS // KV_HEADS
     for h in range(HEADS):
@@ -294,12 +303,14 @@
 
 def attend(queries, keys_cache, values_cache, lengths):
     row_count, cache_span, width = keys_cache.shape
-    vmem = pl.BlockSpec(memory_space=pltpu.VMEM)
     return pl.pallas_call(
         attend_kernel,
-        out_shape=jax.ShapeDtypeStruct(queries.shape, jnp.bfloat16),
-        in_specs=[pl.BlockSpec(memory_space=pltpu.SMEM), vmem, vmem, vmem],
-        out_specs=vmem,
+        out_shape=(
+            jax.ShapeDtypeStruct(queries.shape, jnp.bfloat16),
+            jax.ShapeDtypeStruct((8, 128), jnp.float32),
+        ),
+        in_specs=[SMEM, VMEM, VMEM, VMEM],
+        out_specs=(VMEM, VMEM),
         scratch_shapes=[
             pltpu.VMEM((row_count, HEADS, HEAD_DIM), jnp.float32),
             pltpu.VMEM((row_count, HEADS, HEAD_DIM), jnp.float32),
@@ -339,21 +350,20 @@
         near.append(distance)
         distance *= 2
 
-    depth = w_gate.shape[0]
     normed = normalize(hidden, norm_gain)
-    (gate_low,) = prefetch([(w_gate, 0, depth // 2)], normed, 36)
+    first = prefetch([(w_gate, 0, 3072)], normed, 36)
     blocks = [normed] + [swap(normed, k * group_size) for k in range(1, EXPERTS)]
-    x = merge(blocks, [gate_low])
-    (gate_high,) = prefetch([(w_gate, depth // 2, depth // 2)], x, 36)
-    pieces, after = [x], [gate_high]
+    x = merge(blocks, [first[-1]])
+    second = prefetch([(w_gate, 3072, 3072)], x, 36)
+    pieces, after = [x], [second[-1]]
     for distance in reversed(near):
         arrived = [swap(piece, distance) for piece in pieces]
         if after:
             arrived[0] = merge(arrived[:1], after)
         pieces, after = pieces + arrived, []
-    keep, send = expert_ffn(pieces, (gate_low, gate_high), w_up, w_down)
-
-    context = attend(queries, keys_cache, values_cache, lengths)
+    keep, send = expert_ffn(pieces, first + second, w_up, w_down)
+
+    context, token = attend(queries, keys_cache, values_cache, lengths)
     own_expert = lax.axis_index("pool") // group_size
     order = own_expert ^ jnp.arange(EXPERTS, dtype=jnp.int32)
     named = expert_ids[:, :, None] == order[None, None, :]
@@ -362,7 +372,7 @@
     )
     for distance in near[:-1]:
         keep, send = split_in_two(keep, swap(send, distance))
-    kept, *sent = split_by_expert(keep, swap(send, near[-1]), context)
+    kept, *sent = split_by_expert(keep, swap(send, near[-1]), token)
     received = [swap(block, (k + 1) * group_size) for k, block in enumerate(sent)]
     moe_out = finish(hidden, coefficient, kept, received)
     return (context, moe_out)

time: 60 us -> 57 us (0.950)
  Pallas kernels: 34 us -> 31.8 us
  local copies, waits for them, and re-layouts: 3.11 us -> 2.31 us
    pallas_call x3, Pallas kernels: 22.3 us -> 20 us  [the longest x1 16.4 us: expert_ffn(): pl.pallas_call(functools.partial(ffn_kernel, len(pieces), len(gates)), ou...]
    unnamed x20 -> x18, local copies, waits for them, and re-layouts: 3.11 us -> 2.31 us
  transfers between devices with their start and end apart: 11 -> 11, of which waited for: 8 -> 8; matrix products, arithmetic and copies ran while one was open for 0% -> 0% of each run, Pallas kernels for 21% -> 23%
where the time goes in v3:
time: 57 us; the launch traced here: 56.7 us
  Pallas kernels  31.8 us (56%)
  starting transfers between devices  13.7 us (24%)
  waiting for transfers between devices  8.02 us (14%)
  local copies, waits for them, and re-layouts  2.31 us (4%)
  between operations  0.79 us (1%)
    pallas_call x1, Pallas kernels, expert_ffn(): pl.pallas_call(functools.partial(ffn_kernel, len(pieces), len(gates)), ou...  16.4 us
    ppermute x11, starting transfers between devices, swap(): lax.ppermute(value, 'pool', [(i, i ^ distance) for i in range(devices)])  13.7 us
    pallas_call x2, Pallas kernels, prefetch(): pl.pallas_call(functools.partial(prefetch_kernel, tuple((first for _, fir...  9.17 us
    ppermute x11, waiting for transfers between devices, swap(): lax.ppermute(value, 'pool', [(i, i ^ distance) for i in range(devices)])  8.02 us
    pallas_call x1, Pallas kernels, attend(): pl.pallas_call(attend_kernel, out_shape=(jax.ShapeDtypeStruct(queries.sha...  3.61 us
    unnamed x18, local copies, waits for them, and re-layouts  2.31 us
    pallas_call x1, Pallas kernels, normalize(): pl.pallas_call(norm_kernel, out_shape=jax.ShapeDtypeStruct(hidden.shape,...  1.62 us
  transfers between devices with their start and end apart: 11, of which 8 were waited for; matrix products, arithmetic and copies ran while one was open for 0% of the time, Pallas kernels for 23%

profile of v3, /device:TPU:0, one launch (start us, length us, event | category | flops | bytes accessed | tf_op | source)
XLA Modules:
  0.0 56.7 jit_solution(4687934261330347188)
XLA Ops:
  0.6 1.6 %shard_map.123.refs_1_.refs_0_ = bf16[4,6144]{1,0:T(4,128)(2,1)} custom-call(bf16[4,6144]{1,0:T(4,128)(2,1)} %hidden_ref.1, bf16[6144]{0:T(1024)(128)(2,1)} %gain_hbm.1), custom_call_target="tpu_custom_call" | custom-call | tf_op jit(solution)/shard_map/pallas_call | solution.py:35
  2.3 3.1 %collective-permute-start = (bf16[4,6144]{1,0:T(4,128)(2,1)}, bf16[4,6144]{1,0:T(4,128)(2,1)S(1)}, u32[]{:S(2)}, u32[]{:S(2)}) collective-permute-start(bf16[4,6144]{1,0:T(4,128)(2,1)} %shard_map.123.refs_1_.refs_0_), channel_id=1, source_target_pairs={{0,4},{1,5},{2,6},{3,7},{4,0},{5,1},{6,2},{7,3},{8,12},{9,13},{10,... | collective-permute-start | bytes 147464 | tf_op jit(solution)/shard_map/ppermute | solution.py:345
  5.3 2.6 %collective-permute-start.1 = (bf16[4,6144]{1,0:T(4,128)(2,1)}, bf16[4,6144]{1,0:T(4,128)(2,1)S(1)}, u32[]{:S(2)}, u32[]{:S(2)}) collective-permute-start(bf16[4,6144]{1,0:T(4,128)(2,1)} %shard_map.123.refs_1_.refs_0_), channel_id=1, source_target_pairs={{0,8},{1,9},{2,10},{3,11},{4,12},{5,13},{6,14},{7,15},{8,0},{9,1},... | collective-permute-start | bytes 147464 | tf_op jit(solution)/shard_map/ppermute | solution.py:345
  7.9 0.0 collective-permute-start.2
  7.9 0.0 copy-start.2
  7.9 0.9 %copy-done.2 = bf16[4,6144]{1,0:T(4,128)(2,1)S(1)} copy-done((bf16[4,6144]{1,0:T(4,128)(2,1)S(1)}, bf16[4,6144]{1,0:T(4,128)(2,1)}, u32[]{:S(2)}) %copy-start.2) | copy-done | bytes 49176
  8.8 0.0 copy-start.3
  8.8 4.6 %shard_map.124.refs_4_ = bf16[3072,2048]{1,0:T(8,128)(2,1)S(1)} custom-call(bf16[6144,2048]{1,0:T(8,128)(2,1)} %refs_0_.3, bf16[4,6144]{1,0:T(4,128)(2,1)S(1)} %copy-done.2), custom_call_target="tpu_custom_call" | custom-call | bytes 12582912 | tf_op jit(solution)/shard_map/pallas_call | solution.py:80
  13.4 0.0 collective-permute-done.refs_1_
  13.4 0.0 collective-permute-done.1.refs_2_
  13.4 0.6 %collective-permute-done.2.refs_3_ = bf16[4,6144]{1,0:T(4,128)(2,1)S(1)} collective-permute-done((bf16[4,6144]{1,0:T(4,128)(2,1)}, bf16[4,6144]{1,0:T(4,128)(2,1)S(1)}, u32[]{:S(2)}, u32[]{:S(2)}) %collective-permute-start.2) | collective-permute-done | bytes 49184 | tf_op jit(solution)/shard_map/ppermute | solution.py:345
  14.0 0.0 copy-done.3
  14.0 0.1 shard_map.125.refs_1_.refs_0_
  14.1 1.6 %collective-permute-start.3 = (bf16[16,6144]{1,0:T(8,128)(2,1)S(1)}, bf16[16,6144]{1,0:T(8,128)(2,1)S(1)}, u32[]{:S(2)}, u32[]{:S(2)}) collective-permute-start(bf16[16,6144]{1,0:T(8,128)(2,1)S(1)} %shard_map.125.refs_1_.refs_0_), channel_id=1, source_target_pairs={{0,2},{1,3},{2,0},{3,1},{4,6},{5,7},{6,4},{7,5},{8,10},{9,11},{10,... | collective-permute-start | bytes 589832 | tf_op jit(solution)/shard_map/ppermute | solution.py:345
  15.7 4.6 %shard_map.126.refs_1_.refs_5_ = bf16[3072,2048]{1,0:T(8,128)(2,1)S(1)} custom-call(bf16[6144,2048]{1,0:T(8,128)(2,1)} %refs_0_.3, bf16[16,6144]{1,0:T(8,128)(2,1)S(1)} %shard_map.125.refs_1_.refs_0_), custom_call_target="tpu_custom_call" | custom-call | bytes 12582912 | tf_op jit(solution)/shard_map/pallas_call | solution.py:80
  20.3 0.1 collective-permute-start.4
  20.3 0.0 collective-permute-done.3.refs_0_
  20.4 0.0 copy-start.8
  20.4 0.0 copy-start
  20.4 0.0 copy-start.5
  20.4 0.0 copy-start.6
  20.4 0.0 copy-start.7
  20.4 0.0 copy-start.4
  20.4 0.5 collective-permute-start.5
  21.0 0.8 %collective-permute-done.4.refs_2_ = bf16[16,6144]{1,0:T(8,128)(2,1)S(1)} collective-permute-done((bf16[16,6144]{1,0:T(8,128)(2,1)S(1)}, bf16[16,6144]{1,0:T(8,128)(2,1)S(1)}, u32[]{:S(2)}, u32[]{:S(2)}) %collective-permute-start.4) | collective-permute-done | bytes 196640 | tf_op jit(solution)/shard_map/ppermute | solution.py:345
  21.8 0.3 collective-permute-done.5.refs_3_
  22.1 16.4 %shard_map.128 = (f32[32,6144]{1,0:T(8,128)S(1)}, bf16[32,6144]{1,0:T(8,128)(2,1)S(1)}) custom-call(bf16[16,6144]{1,0:T(8,128)(2,1)S(1)} %shard_map.125.refs_1_.refs_0_, bf16[16,6144]{1,0:T(8,128)(2,1)S(1)} %shard_map.127.refs_1_, bf16[16,6144]{1,0:T(8,128)(2,1)S(1)} %collective-permute-done.4.refs_2_, bf16[16,6144]{1,0:T(8,128)(2,1)S(1)} %collective-permute-done.5.refs_3_, ...), custom_call_target="tpu_custom_call" | custom-call | flops 4831838208 | bytes 75497472 | tf_op jit(solution)/shard_map/pallas_call | solution.py:186
  38.5 0.4 collective-permute-start.6
  38.9 1.4 %collective-permute-done.6.received_ref = bf16[32,6144]{1,0:T(8,128)(2,1)S(1)} collective-permute-done((bf16[32,6144]{1,0:T(8,128)(2,1)S(1)}, bf16[32,6144]{1,0:T(8,128)(2,1)S(1)}, u32[]{:S(2)}, u32[]{:S(2)}) %collective-permute-start.6) | collective-permute-done | bytes 393248 | tf_op jit(solution)/shard_map/ppermute | solution.py:345
  40.2 0.1 shard_map.129
  40.3 0.9 %collective-permute-start.7 = (bf16[16,6144]{1,0:T(8,128)(2,1)S(1)}, bf16[16,6144]{1,0:T(8,128)(2,1)S(1)}, u32[]{:S(2)}, u32[]{:S(2)}) collective-permute-start(bf16[16,6144]{1,0:T(8,128)(2,1)S(1)} %get-tuple-element.16), channel_id=1, source_target_pairs={{0,2},{1,3},{2,0},{3,1},{4,6},{5,7},{6,4},{7,5},{8,10},{9,11},{10,... | collective-permute-start | bytes 589832 | tf_op jit(solution)/shard_map/ppermute | solution.py:345
  41.2 0.0 copy-done.8
  41.3 0.0 copy-done
  41.3 0.0 copy-done.5
  41.3 0.0 copy-done.6
  41.3 0.0 copy-start.1
  41.3 1.4 %copy-done.1 = bf16[4,192,1024]{2,1,0:T(8,128)(2,1)S(1)} copy-done((bf16[4,192,1024]{2,1,0:T(8,128)(2,1)S(1)}, bf16[4,192,1024]{2,1,0:T(8,128)(2,1)}, u32[]{:S(2)}) %copy-start.1) | copy-done | bytes 1572888
  42.7 3.6 %shard_map.122 = (bf16[4,6144]{1,0:T(4,128)(2,1)}, f32[8,128]{1,0:T(8,128)S(1)}) custom-call(s32[4]{0:T(128)S(1)} %copy-done.6, bf16[4,6144]{1,0:T(4,128)(2,1)S(1)} %copy-done.5, bf16[4,192,1024]{2,1,0:T(8,128)(2,1)S(1)} %copy-done, bf16[4,192,1024]{2,1,0:T(8,128)(2,1)S(1)} %copy-done.1), custom_call_target="tpu_custom_call" | custom-call | flops 150994944 | bytes 3145728 | tf_op jit(solution)/shard_map/pallas_call | solution.py:306
  46.3 1.3 %collective-permute-done.7.received_ref = bf16[16,6144]{1,0:T(8,128)(2,1)S(1)} collective-permute-done((bf16[16,6144]{1,0:T(8,128)(2,1)S(1)}, bf16[16,6144]{1,0:T(8,128)(2,1)S(1)}, u32[]{:S(2)}, u32[]{:S(2)}) %collective-permute-start.7) | collective-permute-done | bytes 196640 | tf_op jit(solution)/shard_map/ppermute | solution.py:345
  47.6 0.1 shard_map.130
  47.6 3.3 %collective-permute-start.10 = (bf16[4,6144]{1,0:T(4,128)(2,1)S(1)}, bf16[4,6144]{1,0:T(4,128)(2,1)S(1)}, u32[]{:S(2)}, u32[]{:S(2)}) collective-permute-start(bf16[4,6144]{1,0:T(4,128)(2,1)S(1)} %get-tuple-element.21), channel_id=1, source_target_pairs={{0,12},{1,13},{2,14},{3,15},{4,8},{5,9},{6,10},{7,11},{8,4},{9,5},... | collective-permute-start | bytes 147464 | tf_op jit(solution)/shard_map/ppermute | solution.py:345
  50.9 0.0 collective-permute-start.8
  50.9 1.2 %collective-permute-start.9 = (bf16[4,6144]{1,0:T(4,128)(2,1)S(1)}, bf16[4,6144]{1,0:T(4,128)(2,1)S(1)}, u32[]{:S(2)}, u32[]{:S(2)}) collective-permute-start(bf16[4,6144]{1,0:T(4,128)(2,1)S(1)} %get-tuple-element.20), channel_id=1, source_target_pairs={{0,8},{1,9},{2,10},{3,11},{4,12},{5,13},{6,14},{7,15},{8,0},{9,1},... | collective-permute-start | bytes 147464 | tf_op jit(solution)/shard_map/ppermute | solution.py:345
  52.1 0.0 copy-done.7
  52.1 0.1 select_reduce_fusion.coefficient_ref
  52.1 1.5 %collective-permute-done.10.refs_2_ = bf16[4,6144]{1,0:T(4,128)(2,1)S(1)} collective-permute-done((bf16[4,6144]{1,0:T(4,128)(2,1)S(1)}, bf16[4,6144]{1,0:T(4,128)(2,1)S(1)}, u32[]{:S(2)}, u32[]{:S(2)}) %collective-permute-start.10) | collective-permute-done | bytes 49184 | tf_op jit(solution)/shard_map/ppermute | solution.py:345
  53.7 1.3 %collective-permute-done.8.refs_0_ = bf16[4,6144]{1,0:T(4,128)(2,1)S(1)} collective-permute-done((bf16[4,6144]{1,0:T(4,128)(2,1)S(1)}, bf16[4,6144]{1,0:T(4,128)(2,1)S(1)}, u32[]{:S(2)}, u32[]{:S(2)}) %collective-permute-start.8) | collective-permute-done | bytes 49184 | tf_op jit(solution)/shard_map/ppermute | solution.py:345
  55.0 0.9 %collective-permute-done.9.refs_1_ = bf16[4,6144]{1,0:T(4,128)(2,1)S(1)} collective-permute-done((bf16[4,6144]{1,0:T(4,128)(2,1)S(1)}, bf16[4,6144]{1,0:T(4,128)(2,1)S(1)}, u32[]{:S(2)}, u32[]{:S(2)}) %collective-permute-start.9) | collective-permute-done | bytes 49184 | tf_op jit(solution)/shard_map/ppermute | solution.py:345
  55.9 0.0 copy-done.4
  55.9 0.8 %shard_map.131 = bf16[4,6144]{1,0:T(4,128)(2,1)} custom-call(bf16[4,6144]{1,0:T(4,128)(2,1)S(1)} %copy-done.4, f32[4,4]{1,0:T(4,128)S(1)} %select_reduce_fusion.coefficient_ref, f32[4,6144]{1,0:T(4,128)S(1)} %get-tuple-element.18.kept_ref, bf16[4,6144]{1,0:T(4,128)(2,1)S(1)} %collective-permute-done.8.refs_0_, ...), custom_call_target="tpu_custom_call" | custom-call | tf_op jit(solution)/shard_map/pallas_call | solution.py:263
  (3 shorter events, 0.0 us)
Async XLA Ops:
  2.3 11.2 %collective-permute-start = (bf16[4,6144]{1,0:T(4,128)(2,1)}, bf16[4,6144]{1,0:T(4,128)(2,1)S(1)}, u32[]{:S(2)}, u32[]{:S(2)}) collective-permute-start(bf16[4,6144]{1,0:T(4,128)(2,1)} %shard_map.123.refs_1_.refs_0_), channel_id=1, source_target_pairs={{0,4},{1,5},{2,6},{3,7},{4,0},{5,1},{6,2},{7,3},{8,12},{9,13},{10,... | collective-permute-start | bytes 147464 | tf_op jit(solution)/shard_map/ppermute | solution.py:345
  5.3 8.1 %collective-permute-start.1 = (bf16[4,6144]{1,0:T(4,128)(2,1)}, bf16[4,6144]{1,0:T(4,128)(2,1)S(1)}, u32[]{:S(2)}, u32[]{:S(2)}) collective-permute-start(bf16[4,6144]{1,0:T(4,128)(2,1)} %shard_map.123.refs_1_.refs_0_), channel_id=1, source_target_pairs={{0,8},{1,9},{2,10},{3,11},{4,12},{5,13},{6,14},{7,15},{8,0},{9,1},... | collective-permute-start | bytes 147464 | tf_op jit(solution)/shard_map/ppermute | solution.py:345
  7.9 6.1 %collective-permute-start.2 = (bf16[4,6144]{1,0:T(4,128)(2,1)}, bf16[4,6144]{1,0:T(4,128)(2,1)S(1)}, u32[]{:S(2)}, u32[]{:S(2)}) collective-permute-start(bf16[4,6144]{1,0:T(4,128)(2,1)} %shard_map.123.refs_1_.refs_0_), channel_id=1, source_target_pairs={{0,12},{1,13},{2,14},{3,15},{4,8},{5,9},{6,10},{7,11},{8,4},{9,5},... | collective-permute-start | bytes 147464 | tf_op jit(solution)/shard_map/ppermute | solution.py:345
  7.9 0.9 %copy-start.2 = (bf16[4,6144]{1,0:T(4,128)(2,1)S(1)}, bf16[4,6144]{1,0:T(4,128)(2,1)}, u32[]{:S(2)}) copy-start(bf16[4,6144]{1,0:T(4,128)(2,1)} %shard_map.123.refs_1_.refs_0_) | copy-start | bytes 147460
  8.8 5.2 %copy-start.3 = (bf16[4,6144]{1,0:T(4,128)(2,1)S(1)}, bf16[4,6144]{1,0:T(4,128)(2,1)}, u32[]{:S(2)}) copy-start(bf16[4,6144]{1,0:T(4,128)(2,1)} %shard_map.123.refs_1_.refs_0_) | copy-start | bytes 147460
  14.1 6.2 %collective-permute-start.3 = (bf16[16,6144]{1,0:T(8,128)(2,1)S(1)}, bf16[16,6144]{1,0:T(8,128)(2,1)S(1)}, u32[]{:S(2)}, u32[]{:S(2)}) collective-permute-start(bf16[16,6144]{1,0:T(8,128)(2,1)S(1)} %shard_map.125.refs_1_.refs_0_), channel_id=1, source_target_pairs={{0,2},{1,3},{2,0},{3,1},{4,6},{5,7},{6,4},{7,5},{8,10},{9,11},{10,... | collective-permute-start | bytes 589832 | tf_op jit(solution)/shard_map/ppermute | solution.py:345
  20.3 1.5 %collective-permute-start.4 = (bf16[16,6144]{1,0:T(8,128)(2,1)S(1)}, bf16[16,6144]{1,0:T(8,128)(2,1)S(1)}, u32[]{:S(2)}, u32[]{:S(2)}) collective-permute-start(bf16[16,6144]{1,0:T(8,128)(2,1)S(1)} %shard_map.125.refs_1_.refs_0_), channel_id=1, source_target_pairs={{0,1},{1,0},{2,3},{3,2},{4,5},{5,4},{6,7},{7,6},{8,9},{9,8},{10,11... | collective-permute-start | bytes 589832 | tf_op jit(solution)/shard_map/ppermute | solution.py:345
  20.4 20.9 %copy-start.8 = (bf16[4,2]{0,1:T(2,128)(2,1)S(1)}, bf16[4,2]{0,1:T(2,128)(2,1)}, u32[]{:S(2)}) copy-start(bf16[4,2]{0,1:T(2,128)(2,1)} %param.18) | copy-start | bytes 52
  20.4 20.9 %copy-start = (bf16[4,192,1024]{2,1,0:T(8,128)(2,1)S(1)}, bf16[4,192,1024]{2,1,0:T(8,128)(2,1)}, u32[]{:S(2)}) copy-start(bf16[4,192,1024]{2,1,0:T(8,128)(2,1)} %keys_ref.1) | copy-start | bytes 4718596
  20.4 20.9 %copy-start.5 = (bf16[4,6144]{1,0:T(4,128)(2,1)S(1)}, bf16[4,6144]{1,0:T(4,128)(2,1)}, u32[]{:S(2)}) copy-start(bf16[4,6144]{1,0:T(4,128)(2,1)} %queries_ref.1) | copy-start | bytes 147460
  20.4 20.9 %copy-start.6 = (s32[4]{0:T(128)S(1)}, s32[4]{0:T(128)}, u32[]{:S(2)}) copy-start(s32[4]{0:T(128)} %lengths_ref.1) | copy-start | bytes 52
  20.4 31.7 %copy-start.7 = (s32[4,2]{0,1:T(2,128)S(1)}, s32[4,2]{0,1:T(2,128)}, u32[]{:S(2)}) copy-start(s32[4,2]{0,1:T(2,128)} %param.17) | copy-start | bytes 100
  20.4 35.5 %copy-start.4 = (bf16[4,6144]{1,0:T(4,128)(2,1)S(1)}, bf16[4,6144]{1,0:T(4,128)(2,1)}, u32[]{:S(2)}) copy-start(bf16[4,6144]{1,0:T(4,128)(2,1)} %hidden_ref.1) | copy-start | bytes 147460
  20.4 1.6 %collective-permute-start.5 = (bf16[16,6144]{1,0:T(8,128)(2,1)S(1)}, bf16[16,6144]{1,0:T(8,128)(2,1)S(1)}, u32[]{:S(2)}, u32[]{:S(2)}) collective-permute-start(bf16[16,6144]{1,0:T(8,128)(2,1)S(1)} %shard_map.127.refs_1_), channel_id=1, source_target_pairs={{0,1},{1,0},{2,3},{3,2},{4,5},{5,4},{6,7},{7,6},{8,9},{9,8},{10,11... | collective-permute-start | bytes 589832 | tf_op jit(solution)/shard_map/ppermute | solution.py:345
  38.5 1.8 %collective-permute-start.6 = (bf16[32,6144]{1,0:T(8,128)(2,1)S(1)}, bf16[32,6144]{1,0:T(8,128)(2,1)S(1)}, u32[]{:S(2)}, u32[]{:S(2)}) collective-permute-start(bf16[32,6144]{1,0:T(8,128)(2,1)S(1)} %get-tuple-element.14), channel_id=1, source_target_pairs={{0,1},{1,0},{2,3},{3,2},{4,5},{5,4},{6,7},{7,6},{8,9},{9,8},{10,11... | collective-permute-start | bytes 1179656 | tf_op jit(solution)/shard_map/ppermute | solution.py:345
  40.3 7.2 %collective-permute-start.7 = (bf16[16,6144]{1,0:T(8,128)(2,1)S(1)}, bf16[16,6144]{1,0:T(8,128)(2,1)S(1)}, u32[]{:S(2)}, u32[]{:S(2)}) collective-permute-start(bf16[16,6144]{1,0:T(8,128)(2,1)S(1)} %get-tuple-element.16), channel_id=1, source_target_pairs={{0,2},{1,3},{2,0},{3,1},{4,6},{5,7},{6,4},{7,5},{8,10},{9,11},{10,... | collective-permute-start | bytes 589832 | tf_op jit(solution)/shard_map/ppermute | solution.py:345
  41.3 1.4 %copy-start.1 = (bf16[4,192,1024]{2,1,0:T(8,128)(2,1)S(1)}, bf16[4,192,1024]{2,1,0:T(8,128)(2,1)}, u32[]{:S(2)}) copy-start(bf16[4,192,1024]{2,1,0:T(8,128)(2,1)} %values_ref.1) | copy-start | bytes 4718596
  47.6 6.1 %collective-permute-start.10 = (bf16[4,6144]{1,0:T(4,128)(2,1)S(1)}, bf16[4,6144]{1,0:T(4,128)(2,1)S(1)}, u32[]{:S(2)}, u32[]{:S(2)}) collective-permute-start(bf16[4,6144]{1,0:T(4,128)(2,1)S(1)} %get-tuple-element.21), channel_id=1, source_target_pairs={{0,12},{1,13},{2,14},{3,15},{4,8},{5,9},{6,10},{7,11},{8,4},{9,5},... | collective-permute-start | bytes 147464 | tf_op jit(solution)/shard_map/ppermute | solution.py:345
  50.9 4.1 %collective-permute-start.8 = (bf16[4,6144]{1,0:T(4,128)(2,1)S(1)}, bf16[4,6144]{1,0:T(4,128)(2,1)S(1)}, u32[]{:S(2)}, u32[]{:S(2)}) collective-permute-start(bf16[4,6144]{1,0:T(4,128)(2,1)S(1)} %get-tuple-element.19), channel_id=1, source_target_pairs={{0,4},{1,5},{2,6},{3,7},{4,0},{5,1},{6,2},{7,3},{8,12},{9,13},{10,... | collective-permute-start | bytes 147464 | tf_op jit(solution)/shard_map/ppermute | solution.py:345
  50.9 5.0 %collective-permute-start.9 = (bf16[4,6144]{1,0:T(4,128)(2,1)S(1)}, bf16[4,6144]{1,0:T(4,128)(2,1)S(1)}, u32[]{:S(2)}, u32[]{:S(2)}) collective-permute-start(bf16[4,6144]{1,0:T(4,128)(2,1)S(1)} %get-tuple-element.20), channel_id=1, source_target_pairs={{0,8},{1,9},{2,10},{3,11},{4,12},{5,13},{6,14},{7,15},{8,0},{9,1},... | collective-permute-start | bytes 147464 | tf_op jit(solution)/shard_map/ppermute | solution.py:345

commit v4 on v3

--- a/solution.py
+++ b/solution.py
@@ -34,7 +34,7 @@
 def normalize(hidden, norm_gain):
     return pl.pallas_call(
         norm_kernel,
-        out_shape=jax.ShapeDtypeStruct(hidden.shape, jnp.bfloat16),
+        out_shape=pltpu.VMEM(hidden.shape, jnp.bfloat16),
         in_specs=[HBM, HBM],
         out_specs=VMEM,
         scratch_shapes=[

time: 57 us -> 55.5 us (0.974)
  local copies, waits for them, and re-layouts: 2.31 us -> 1.44 us
  Pallas kernels: 31.8 us -> 31.1 us
    unnamed x18 -> x14, local copies, waits for them, and re-layouts: 2.31 us -> 1.44 us
    pallas_call x1, Pallas kernels: 1.62 us -> 1 us  [normalize(): pl.pallas_call(norm_kernel, out_shape=pltpu.VMEM(hidden.shape, jnp.bfloat...]
where the time goes in v4:
time: 55.5 us; the launch traced here: 55.2 us
  Pallas kernels  31.1 us (56%)
  starting transfers between devices  13.7 us (25%)
  waiting for transfers between devices  8.05 us (15%)
  local copies, waits for them, and re-layouts  1.44 us (3%)
  between operations  0.79 us (1%)
    pallas_call x1, Pallas kernels, expert_ffn(): pl.pallas_call(functools.partial(ffn_kernel, len(pieces), len(gates)), ou...  16.4 us
    ppermute x11, starting transfers between devices, swap(): lax.ppermute(value, 'pool', [(i, i ^ distance) for i in range(devices)])  13.7 us
    pallas_call x2, Pallas kernels, prefetch(): pl.pallas_call(functools.partial(prefetch_kernel, tuple((first for _, fir...  9.17 us
    ppermute x11, waiting for transfers between devices, swap(): lax.ppermute(value, 'pool', [(i, i ^ distance) for i in range(devices)])  8.05 us
    pallas_call x1, Pallas kernels, attend(): pl.pallas_call(attend_kernel, out_shape=(jax.ShapeDtypeStruct(queries.sha...  3.62 us
    unnamed x14, local copies, waits for them, and re-layouts  1.44 us
  transfers between devices with their start and end apart: 11, of which 8 were waited for; matrix products, arithmetic and copies ran while one was open for 0% of the time, Pallas kernels for 23%

profile of v4, /device:TPU:0, one launch (start us, length us, event | category | flops | bytes accessed | tf_op | source)
XLA Modules:
  0.0 55.2 jit_solution(5687826677338271506)
XLA Ops:
  0.6 1.0 %shard_map.123.refs_1_.refs_0_ = bf16[4,6144]{1,0:T(4,128)(2,1)S(1)} custom-call(bf16[4,6144]{1,0:T(4,128)(2,1)} %hidden_ref.1, bf16[6144]{0:T(1024)(128)(2,1)} %gain_hbm.1), custom_call_target="tpu_custom_call" | custom-call | tf_op jit(solution)/shard_map/pallas_call | solution.py:35
  1.6 3.1 %collective-permute-start = (bf16[4,6144]{1,0:T(4,128)(2,1)S(1)}, bf16[4,6144]{1,0:T(4,128)(2,1)S(1)}, u32[]{:S(2)}, u32[]{:S(2)}) collective-permute-start(bf16[4,6144]{1,0:T(4,128)(2,1)S(1)} %shard_map.123.refs_1_.refs_0_), channel_id=1, source_target_pairs={{0,4},{1,5},{2,6},{3,7},{4,0},{5,1},{6,2},{7,3},{8,12},{9,13},{10,... | collective-permute-start | bytes 147464 | tf_op jit(solution)/shard_map/ppermute | solution.py:345
  4.7 2.6 %collective-permute-start.1 = (bf16[4,6144]{1,0:T(4,128)(2,1)S(1)}, bf16[4,6144]{1,0:T(4,128)(2,1)S(1)}, u32[]{:S(2)}, u32[]{:S(2)}) collective-permute-start(bf16[4,6144]{1,0:T(4,128)(2,1)S(1)} %shard_map.123.refs_1_.refs_0_), channel_id=1, source_target_pairs={{0,8},{1,9},{2,10},{3,11},{4,12},{5,13},{6,14},{7,15},{8,0},{9,1},... | collective-permute-start | bytes 147464 | tf_op jit(solution)/shard_map/ppermute | solution.py:345
  7.3 0.0 collective-permute-start.2
  7.3 4.6 %shard_map.124.refs_4_ = bf16[3072,2048]{1,0:T(8,128)(2,1)S(1)} custom-call(bf16[6144,2048]{1,0:T(8,128)(2,1)} %refs_0_.3, bf16[4,6144]{1,0:T(4,128)(2,1)S(1)} %shard_map.123.refs_1_.refs_0_), custom_call_target="tpu_custom_call" | custom-call | bytes 12582912 | tf_op jit(solution)/shard_map/pallas_call | solution.py:80
  11.9 0.0 collective-permute-done.refs_1_
  11.9 0.0 collective-permute-done.1.refs_2_
  11.9 1.3 %collective-permute-done.2.refs_3_ = bf16[4,6144]{1,0:T(4,128)(2,1)S(1)} collective-permute-done((bf16[4,6144]{1,0:T(4,128)(2,1)S(1)}, bf16[4,6144]{1,0:T(4,128)(2,1)S(1)}, u32[]{:S(2)}, u32[]{:S(2)}) %collective-permute-start.2) | collective-permute-done | bytes 49184 | tf_op jit(solution)/shard_map/ppermute | solution.py:345
  13.2 0.1 shard_map.125.refs_1_.refs_0_
  13.3 1.6 %collective-permute-start.3 = (bf16[16,6144]{1,0:T(8,128)(2,1)S(1)}, bf16[16,6144]{1,0:T(8,128)(2,1)S(1)}, u32[]{:S(2)}, u32[]{:S(2)}) collective-permute-start(bf16[16,6144]{1,0:T(8,128)(2,1)S(1)} %shard_map.125.refs_1_.refs_0_), channel_id=1, source_target_pairs={{0,2},{1,3},{2,0},{3,1},{4,6},{5,7},{6,4},{7,5},{8,10},{9,11},{10,... | collective-permute-start | bytes 589832 | tf_op jit(solution)/shard_map/ppermute | solution.py:345
  14.8 4.6 %shard_map.126.refs_1_.refs_5_ = bf16[3072,2048]{1,0:T(8,128)(2,1)S(1)} custom-call(bf16[6144,2048]{1,0:T(8,128)(2,1)} %refs_0_.3, bf16[16,6144]{1,0:T(8,128)(2,1)S(1)} %shard_map.125.refs_1_.refs_0_), custom_call_target="tpu_custom_call" | custom-call | bytes 12582912 | tf_op jit(solution)/shard_map/pallas_call | solution.py:80
  19.4 0.1 collective-permute-start.4
  19.5 0.0 collective-permute-done.3.refs_0_
  19.5 0.0 copy-start.6
  19.5 0.0 copy-start
  19.6 0.0 copy-start.3
  19.6 0.0 copy-start.4
  19.6 0.0 copy-start.5
  19.6 0.0 copy-start.2
  19.6 0.5 collective-permute-start.5
  20.2 0.8 %collective-permute-done.4.refs_2_ = bf16[16,6144]{1,0:T(8,128)(2,1)S(1)} collective-permute-done((bf16[16,6144]{1,0:T(8,128)(2,1)S(1)}, bf16[16,6144]{1,0:T(8,128)(2,1)S(1)}, u32[]{:S(2)}, u32[]{:S(2)}) %collective-permute-start.4) | collective-permute-done | bytes 196640 | tf_op jit(solution)/shard_map/ppermute | solution.py:345
  20.9 0.3 collective-permute-done.5.refs_3_
  21.2 16.4 %shard_map.128 = (f32[32,6144]{1,0:T(8,128)S(1)}, bf16[32,6144]{1,0:T(8,128)(2,1)S(1)}) custom-call(bf16[16,6144]{1,0:T(8,128)(2,1)S(1)} %shard_map.125.refs_1_.refs_0_, bf16[16,6144]{1,0:T(8,128)(2,1)S(1)} %shard_map.127.refs_1_, bf16[16,6144]{1,0:T(8,128)(2,1)S(1)} %collective-permute-done.4.refs_2_, bf16[16,6144]{1,0:T(8,128)(2,1)S(1)} %collective-permute-done.5.refs_3_, ...), custom_call_target="tpu_custom_call" | custom-call | flops 4831838208 | bytes 75497472 | tf_op jit(solution)/shard_map/pallas_call | solution.py:186
  37.6 0.4 collective-permute-start.6
  38.1 1.4 %collective-permute-done.6.received_ref = bf16[32,6144]{1,0:T(8,128)(2,1)S(1)} collective-permute-done((bf16[32,6144]{1,0:T(8,128)(2,1)S(1)}, bf16[32,6144]{1,0:T(8,128)(2,1)S(1)}, u32[]{:S(2)}, u32[]{:S(2)}) %collective-permute-start.6) | collective-permute-done | bytes 393248 | tf_op jit(solution)/shard_map/ppermute | solution.py:345
  39.4 0.1 shard_map.129
  39.5 0.9 %collective-permute-start.7 = (bf16[16,6144]{1,0:T(8,128)(2,1)S(1)}, bf16[16,6144]{1,0:T(8,128)(2,1)S(1)}, u32[]{:S(2)}, u32[]{:S(2)}) collective-permute-start(bf16[16,6144]{1,0:T(8,128)(2,1)S(1)} %get-tuple-element.16), channel_id=1, source_target_pairs={{0,2},{1,3},{2,0},{3,1},{4,6},{5,7},{6,4},{7,5},{8,10},{9,11},{10,... | collective-permute-start | bytes 589832 | tf_op jit(solution)/shard_map/ppermute | solution.py:345
  40.4 0.0 copy-done.6
  40.4 0.0 copy-done
  40.4 0.0 copy-done.3
  40.4 0.0 copy-done.4
  40.4 0.0 copy-start.1
  40.4 1.4 %copy-done.1 = bf16[4,192,1024]{2,1,0:T(8,128)(2,1)S(1)} copy-done((bf16[4,192,1024]{2,1,0:T(8,128)(2,1)S(1)}, bf16[4,192,1024]{2,1,0:T(8,128)(2,1)}, u32[]{:S(2)}) %copy-start.1) | copy-done | bytes 1572888
  41.8 3.6 %shard_map.122 = (bf16[4,6144]{1,0:T(4,128)(2,1)}, f32[8,128]{1,0:T(8,128)S(1)}) custom-call(s32[4]{0:T(128)S(1)} %copy-done.4, bf16[4,6144]{1,0:T(4,128)(2,1)S(1)} %copy-done.3, bf16[4,192,1024]{2,1,0:T(8,128)(2,1)S(1)} %copy-done, bf16[4,192,1024]{2,1,0:T(8,128)(2,1)S(1)} %copy-done.1), custom_call_target="tpu_custom_call" | custom-call | flops 150994944 | bytes 3145728 | tf_op jit(solution)/shard_map/pallas_call | solution.py:306
  45.5 1.3 %collective-permute-done.7.received_ref = bf16[16,6144]{1,0:T(8,128)(2,1)S(1)} collective-permute-done((bf16[16,6144]{1,0:T(8,128)(2,1)S(1)}, bf16[16,6144]{1,0:T(8,128)(2,1)S(1)}, u32[]{:S(2)}, u32[]{:S(2)}) %collective-permute-start.7) | collective-permute-done | bytes 196640 | tf_op jit(solution)/shard_map/ppermute | solution.py:345
  46.7 0.1 shard_map.130
  46.8 2.6 %collective-permute-start.10 = (bf16[4,6144]{1,0:T(4,128)(2,1)S(1)}, bf16[4,6144]{1,0:T(4,128)(2,1)S(1)}, u32[]{:S(2)}, u32[]{:S(2)}) collective-permute-start(bf16[4,6144]{1,0:T(4,128)(2,1)S(1)} %get-tuple-element.21), channel_id=1, source_target_pairs={{0,12},{1,13},{2,14},{3,15},{4,8},{5,9},{6,10},{7,11},{8,4},{9,5},... | collective-permute-start | bytes 147464 | tf_op jit(solution)/shard_map/ppermute | solution.py:345
  49.4 0.0 collective-permute-start.8
  49.4 1.8 %collective-permute-start.9 = (bf16[4,6144]{1,0:T(4,128)(2,1)S(1)}, bf16[4,6144]{1,0:T(4,128)(2,1)S(1)}, u32[]{:S(2)}, u32[]{:S(2)}) collective-permute-start(bf16[4,6144]{1,0:T(4,128)(2,1)S(1)} %get-tuple-element.20), channel_id=1, source_target_pairs={{0,8},{1,9},{2,10},{3,11},{4,12},{5,13},{6,14},{7,15},{8,0},{9,1},... | collective-permute-start | bytes 147464 | tf_op jit(solution)/shard_map/ppermute | solution.py:345
  51.2 0.0 copy-done.5
  51.2 0.1 select_reduce_fusion.coefficient_ref
  51.3 1.5 %collective-permute-done.10.refs_2_ = bf16[4,6144]{1,0:T(4,128)(2,1)S(1)} collective-permute-done((bf16[4,6144]{1,0:T(4,128)(2,1)S(1)}, bf16[4,6144]{1,0:T(4,128)(2,1)S(1)}, u32[]{:S(2)}, u32[]{:S(2)}) %collective-permute-start.10) | collective-permute-done | bytes 49184 | tf_op jit(solution)/shard_map/ppermute | solution.py:345
  52.8 0.9 %collective-permute-done.8.refs_0_ = bf16[4,6144]{1,0:T(4,128)(2,1)S(1)} collective-permute-done((bf16[4,6144]{1,0:T(4,128)(2,1)S(1)}, bf16[4,6144]{1,0:T(4,128)(2,1)S(1)}, u32[]{:S(2)}, u32[]{:S(2)}) %collective-permute-start.8) | collective-permute-done | bytes 49184 | tf_op jit(solution)/shard_map/ppermute | solution.py:345
  53.8 0.7 %collective-permute-done.9.refs_1_ = bf16[4,6144]{1,0:T(4,128)(2,1)S(1)} collective-permute-done((bf16[4,6144]{1,0:T(4,128)(2,1)S(1)}, bf16[4,6144]{1,0:T(4,128)(2,1)S(1)}, u32[]{:S(2)}, u32[]{:S(2)}) %collective-permute-start.9) | collective-permute-done | bytes 49184 | tf_op jit(solution)/shard_map/ppermute | solution.py:345
  54.4 0.0 copy-done.2
  54.4 0.8 %shard_map.131 = bf16[4,6144]{1,0:T(4,128)(2,1)} custom-call(bf16[4,6144]{1,0:T(4,128)(2,1)S(1)} %copy-done.2, f32[4,4]{1,0:T(4,128)S(1)} %select_reduce_fusion.coefficient_ref, f32[4,6144]{1,0:T(4,128)S(1)} %get-tuple-element.18.kept_ref, bf16[4,6144]{1,0:T(4,128)(2,1)S(1)} %collective-permute-done.8.refs_0_, ...), custom_call_target="tpu_custom_call" | custom-call | tf_op jit(solution)/shard_map/pallas_call | solution.py:263
  (3 shorter events, 0.0 us)
Async XLA Ops:
  1.6 10.3 %collective-permute-start = (bf16[4,6144]{1,0:T(4,128)(2,1)S(1)}, bf16[4,6144]{1,0:T(4,128)(2,1)S(1)}, u32[]{:S(2)}, u32[]{:S(2)}) collective-permute-start(bf16[4,6144]{1,0:T(4,128)(2,1)S(1)} %shard_map.123.refs_1_.refs_0_), channel_id=1, source_target_pairs={{0,4},{1,5},{2,6},{3,7},{4,0},{5,1},{6,2},{7,3},{8,12},{9,13},{10,... | collective-permute-start | bytes 147464 | tf_op jit(solution)/shard_map/ppermute | solution.py:345
  4.7 7.2 %collective-permute-start.1 = (bf16[4,6144]{1,0:T(4,128)(2,1)S(1)}, bf16[4,6144]{1,0:T(4,128)(2,1)S(1)}, u32[]{:S(2)}, u32[]{:S(2)}) collective-permute-start(bf16[4,6144]{1,0:T(4,128)(2,1)S(1)} %shard_map.123.refs_1_.refs_0_), channel_id=1, source_target_pairs={{0,8},{1,9},{2,10},{3,11},{4,12},{5,13},{6,14},{7,15},{8,0},{9,1},... | collective-permute-start | bytes 147464 | tf_op jit(solution)/shard_map/ppermute | solution.py:345
  7.3 5.9 %collective-permute-start.2 = (bf16[4,6144]{1,0:T(4,128)(2,1)S(1)}, bf16[4,6144]{1,0:T(4,128)(2,1)S(1)}, u32[]{:S(2)}, u32[]{:S(2)}) collective-permute-start(bf16[4,6144]{1,0:T(4,128)(2,1)S(1)} %shard_map.123.refs_1_.refs_0_), channel_id=1, source_target_pairs={{0,12},{1,13},{2,14},{3,15},{4,8},{5,9},{6,10},{7,11},{8,4},{9,5},... | collective-permute-start | bytes 147464 | tf_op jit(solution)/shard_map/ppermute | solution.py:345
  13.3 6.2 %collective-permute-start.3 = (bf16[16,6144]{1,0:T(8,128)(2,1)S(1)}, bf16[16,6144]{1,0:T(8,128)(2,1)S(1)}, u32[]{:S(2)}, u32[]{:S(2)}) collective-permute-start(bf16[16,6144]{1,0:T(8,128)(2,1)S(1)} %shard_map.125.refs_1_.refs_0_), channel_id=1, source_target_pairs={{0,2},{1,3},{2,0},{3,1},{4,6},{5,7},{6,4},{7,5},{8,10},{9,11},{10,... | collective-permute-start | bytes 589832 | tf_op jit(solution)/shard_map/ppermute | solution.py:345
  19.4 1.5 %collective-permute-start.4 = (bf16[16,6144]{1,0:T(8,128)(2,1)S(1)}, bf16[16,6144]{1,0:T(8,128)(2,1)S(1)}, u32[]{:S(2)}, u32[]{:S(2)}) collective-permute-start(bf16[16,6144]{1,0:T(8,128)(2,1)S(1)} %shard_map.125.refs_1_.refs_0_), channel_id=1, source_target_pairs={{0,1},{1,0},{2,3},{3,2},{4,5},{5,4},{6,7},{7,6},{8,9},{9,8},{10,11... | collective-permute-start | bytes 589832 | tf_op jit(solution)/shard_map/ppermute | solution.py:345
  19.5 20.9 %copy-start.6 = (bf16[4,2]{0,1:T(2,128)(2,1)S(1)}, bf16[4,2]{0,1:T(2,128)(2,1)}, u32[]{:S(2)}) copy-start(bf16[4,2]{0,1:T(2,128)(2,1)} %param.18) | copy-start | bytes 52
  19.5 20.9 %copy-start = (bf16[4,192,1024]{2,1,0:T(8,128)(2,1)S(1)}, bf16[4,192,1024]{2,1,0:T(8,128)(2,1)}, u32[]{:S(2)}) copy-start(bf16[4,192,1024]{2,1,0:T(8,128)(2,1)} %keys_ref.1) | copy-start | bytes 4718596
  19.6 20.9 %copy-start.3 = (bf16[4,6144]{1,0:T(4,128)(2,1)S(1)}, bf16[4,6144]{1,0:T(4,128)(2,1)}, u32[]{:S(2)}) copy-start(bf16[4,6144]{1,0:T(4,128)(2,1)} %queries_ref.1) | copy-start | bytes 147460
  19.6 20.9 %copy-start.4 = (s32[4]{0:T(128)S(1)}, s32[4]{0:T(128)}, u32[]{:S(2)}) copy-start(s32[4]{0:T(128)} %lengths_ref.1) | copy-start | bytes 52
  19.6 31.6 %copy-start.5 = (s32[4,2]{0,1:T(2,128)S(1)}, s32[4,2]{0,1:T(2,128)}, u32[]{:S(2)}) copy-start(s32[4,2]{0,1:T(2,128)} %param.17) | copy-start | bytes 100
  19.6 34.8 %copy-start.2 = (bf16[4,6144]{1,0:T(4,128)(2,1)S(1)}, bf16[4,6144]{1,0:T(4,128)(2,1)}, u32[]{:S(2)}) copy-start(bf16[4,6144]{1,0:T(4,128)(2,1)} %hidden_ref.1) | copy-start | bytes 147460
  19.6 1.6 %collective-permute-start.5 = (bf16[16,6144]{1,0:T(8,128)(2,1)S(1)}, bf16[16,6144]{1,0:T(8,128)(2,1)S(1)}, u32[]{:S(2)}, u32[]{:S(2)}) collective-permute-start(bf16[16,6144]{1,0:T(8,128)(2,1)S(1)} %shard_map.127.refs_1_), channel_id=1, source_target_pairs={{0,1},{1,0},{2,3},{3,2},{4,5},{5,4},{6,7},{7,6},{8,9},{9,8},{10,11... | collective-permute-start | bytes 589832 | tf_op jit(solution)/shard_map/ppermute | solution.py:345
  37.6 1.8 %collective-permute-start.6 = (bf16[32,6144]{1,0:T(8,128)(2,1)S(1)}, bf16[32,6144]{1,0:T(8,128)(2,1)S(1)}, u32[]{:S(2)}, u32[]{:S(2)}) collective-permute-start(bf16[32,6144]{1,0:T(8,128)(2,1)S(1)} %get-tuple-element.14), channel_id=1, source_target_pairs={{0,1},{1,0},{2,3},{3,2},{4,5},{5,4},{6,7},{7,6},{8,9},{9,8},{10,11... | collective-permute-start | bytes 1179656 | tf_op jit(solution)/shard_map/ppermute | solution.py:345
  39.5 7.2 %collective-permute-start.7 = (bf16[16,6144]{1,0:T(8,128)(2,1)S(1)}, bf16[16,6144]{1,0:T(8,128)(2,1)S(1)}, u32[]{:S(2)}, u32[]{:S(2)}) collective-permute-start(bf16[16,6144]{1,0:T(8,128)(2,1)S(1)} %get-tuple-element.16), channel_id=1, source_target_pairs={{0,2},{1,3},{2,0},{3,1},{4,6},{5,7},{6,4},{7,5},{8,10},{9,11},{10,... | collective-permute-start | bytes 589832 | tf_op jit(solution)/shard_map/ppermute | solution.py:345
  40.4 1.4 %copy-start.1 = (bf16[4,192,1024]{2,1,0:T(8,128)(2,1)S(1)}, bf16[4,192,1024]{2,1,0:T(8,128)(2,1)}, u32[]{:S(2)}) copy-start(bf16[4,192,1024]{2,1,0:T(8,128)(2,1)} %values_ref.1) | copy-start | bytes 4718596
  46.8 6.1 %collective-permute-start.10 = (bf16[4,6144]{1,0:T(4,128)(2,1)S(1)}, bf16[4,6144]{1,0:T(4,128)(2,1)S(1)}, u32[]{:S(2)}, u32[]{:S(2)}) collective-permute-start(bf16[4,6144]{1,0:T(4,128)(2,1)S(1)} %get-tuple-element.21), channel_id=1, source_target_pairs={{0,12},{1,13},{2,14},{3,15},{4,8},{5,9},{6,10},{7,11},{8,4},{9,5},... | collective-permute-start | bytes 147464 | tf_op jit(solution)/shard_map/ppermute | solution.py:345
  49.4 4.4 %collective-permute-start.8 = (bf16[4,6144]{1,0:T(4,128)(2,1)S(1)}, bf16[4,6144]{1,0:T(4,128)(2,1)S(1)}, u32[]{:S(2)}, u32[]{:S(2)}) collective-permute-start(bf16[4,6144]{1,0:T(4,128)(2,1)S(1)} %get-tuple-element.19), channel_id=1, source_target_pairs={{0,4},{1,5},{2,6},{3,7},{4,0},{5,1},{6,2},{7,3},{8,12},{9,13},{10,... | collective-permute-start | bytes 147464 | tf_op jit(solution)/shard_map/ppermute | solution.py:345
  49.4 5.0 %collective-permute-start.9 = (bf16[4,6144]{1,0:T(4,128)(2,1)S(1)}, bf16[4,6144]{1,0:T(4,128)(2,1)S(1)}, u32[]{:S(2)}, u32[]{:S(2)}) collective-permute-start(bf16[4,6144]{1,0:T(4,128)(2,1)S(1)} %get-tuple-element.20), channel_id=1, source_target_pairs={{0,8},{1,9},{2,10},{3,11},{4,12},{5,13},{6,14},{7,15},{8,0},{9,1},... | collective-permute-start | bytes 147464 | tf_op jit(solution)/shard_map/ppermute | solution.py:345

commit v5 on v4

--- a/solution.py
+++ b/solution.py
@@ -135,13 +135,13 @@
     gate_sum[...] = jnp.zeros_like(gate_sum)
     up_sum[...] = jnp.zeros_like(up_sum)
 
-    gate_depth = 1024
     offset = 0
     for part in gates:
+        gate_depth = part.shape[0] // 2
 
         @pl.loop(0, part.shape[0] // gate_depth)
         def _(step):
-            columns = pl.ds(pl.multiple_of(offset + step * gate_depth, gate_depth), gate_depth)
+            columns = pl.ds(pl.multiple_of(offset + step * gate_depth, 256), gate_depth)
             gate_sum[...] += jnp.dot(
                 x[:, columns], part[block(step, gate_depth), :], preferred_element_type=jnp.float32
             )
@@ -182,7 +182,7 @@
 def expert_ffn(pieces, gates, w_up, w_down):
     rows = sum(piece.shape[0] for piece in pieces)
     model_width, units = w_up.shape
-    ring, depth = 10, min(512, units)
+    ring, depth = 9, min(512, units)
     return pl.pallas_call(
         functools.partial(ffn_kernel, len(pieces), len(gates)),
         out_shape=(
@@ -199,7 +199,7 @@
             pltpu.VMEM((rows, units), jnp.bfloat16),
             pltpu.SemaphoreType.DMA((ring,)),
         ],
-        compiler_params=pltpu.CompilerParams(vmem_limit_bytes=24 * MIB),
+        compiler_params=pltpu.CompilerParams(vmem_limit_bytes=22 * MIB),
         cost_estimate=pl.CostEstimate(
             flops=6 * rows * model_width * units,
             bytes_accessed=6 * model_width * units,
@@ -351,10 +351,10 @@
         distance *= 2
 
     normed = normalize(hidden, norm_gain)
-    first = prefetch([(w_gate, 0, 3072)], normed, 36)
+    first = prefetch([(w_gate, 0, 3584)], normed, 36)
     blocks = [normed] + [swap(normed, k * group_size) for k in range(1, EXPERTS)]
     x = merge(blocks, [first[-1]])
-    second = prefetch([(w_gate, 3072, 3072)], x, 36)
+    second = prefetch([(w_gate, 3584, 2560)], x, 24)
     pieces, after = [x], [second[-1]]
     for distance in reversed(near):
         arrived = [swap(piece, distance) for piece in pieces]

time: 55.5 us -> 55.3 us (level)
  transfers between devices with their start and end apart: 11 -> 11, of which waited for: 8 -> 9; matrix products, arithmetic and copies ran while one was open for 0% -> 0% of each run, Pallas kernels for 23% -> 23%
where the time goes in v5:
time: 55.3 us; the launch traced here: 55 us
  Pallas kernels  31 us (56%)
  starting transfers between devices  14.2 us (26%)
  waiting for transfers between devices  7.54 us (14%)
  local copies, waits for them, and re-layouts  1.44 us (3%)
  between operations  0.78 us (1%)
    pallas_call x1, Pallas kernels, expert_ffn(): pl.pallas_call(functools.partial(ffn_kernel, len(pieces), len(gates)), ou...  16.2 us
    ppermute x11, starting transfers between devices, swap(): lax.ppermute(value, 'pool', [(i, i ^ distance) for i in range(devices)])  14.2 us
    pallas_call x2, Pallas kernels, prefetch(): pl.pallas_call(functools.partial(prefetch_kernel, tuple((first for _, fir...  9.17 us
    ppermute x11, waiting for transfers between devices, swap(): lax.ppermute(value, 'pool', [(i, i ^ distance) for i in range(devices)])  7.54 us
    pallas_call x1, Pallas kernels, attend(): pl.pallas_call(attend_kernel, out_shape=(jax.ShapeDtypeStruct(queries.sha...  3.62 us
    unnamed x14, local copies, waits for them, and re-layouts  1.44 us
  transfers between devices with their start and end apart: 11, of which 9 were waited for; matrix products, arithmetic and copies ran while one was open for 0% of the time, Pallas kernels for 23%

profile of v5, /device:TPU:0, one launch (start us, length us, event | category | flops | bytes accessed | tf_op | source)
XLA Modules:
  0.0 55.0 jit_solution(9300471897958650885)
XLA Ops:
  0.6 1.0 %shard_map.123.refs_1_.refs_0_ = bf16[4,6144]{1,0:T(4,128)(2,1)S(1)} custom-call(bf16[4,6144]{1,0:T(4,128)(2,1)} %hidden_ref.1, bf16[6144]{0:T(1024)(128)(2,1)} %gain_hbm.1), custom_call_target="tpu_custom_call" | custom-call | tf_op jit(solution)/shard_map/pallas_call | solution.py:35
  1.6 3.1 %collective-permute-start = (bf16[4,6144]{1,0:T(4,128)(2,1)S(1)}, bf16[4,6144]{1,0:T(4,128)(2,1)S(1)}, u32[]{:S(2)}, u32[]{:S(2)}) collective-permute-start(bf16[4,6144]{1,0:T(4,128)(2,1)S(1)} %shard_map.123.refs_1_.refs_0_), channel_id=1, source_target_pairs={{0,4},{1,5},{2,6},{3,7},{4,0},{5,1},{6,2},{7,3},{8,12},{9,13},{10,... | collective-permute-start | bytes 147464 | tf_op jit(solution)/shard_map/ppermute | solution.py:345
  4.7 2.6 %collective-permute-start.1 = (bf16[4,6144]{1,0:T(4,128)(2,1)S(1)}, bf16[4,6144]{1,0:T(4,128)(2,1)S(1)}, u32[]{:S(2)}, u32[]{:S(2)}) collective-permute-start(bf16[4,6144]{1,0:T(4,128)(2,1)S(1)} %shard_map.123.refs_1_.refs_0_), channel_id=1, source_target_pairs={{0,8},{1,9},{2,10},{3,11},{4,12},{5,13},{6,14},{7,15},{8,0},{9,1},... | collective-permute-start | bytes 147464 | tf_op jit(solution)/shard_map/ppermute | solution.py:345
  7.3 0.0 collective-permute-start.2
  7.3 5.2 %shard_map.124.refs_4_ = bf16[3584,2048]{1,0:T(8,128)(2,1)S(1)} custom-call(bf16[6144,2048]{1,0:T(8,128)(2,1)} %refs_0_.3, bf16[4,6144]{1,0:T(4,128)(2,1)S(1)} %shard_map.123.refs_1_.refs_0_), custom_call_target="tpu_custom_call" | custom-call | bytes 14680064 | tf_op jit(solution)/shard_map/pallas_call | solution.py:80
  12.5 0.0 collective-permute-done.refs_1_
  12.5 0.0 collective-permute-done.1.refs_2_
  12.5 0.7 %collective-permute-done.2.refs_3_ = bf16[4,6144]{1,0:T(4,128)(2,1)S(1)} collective-permute-done((bf16[4,6144]{1,0:T(4,128)(2,1)S(1)}, bf16[4,6144]{1,0:T(4,128)(2,1)S(1)}, u32[]{:S(2)}, u32[]{:S(2)}) %collective-permute-start.2) | collective-permute-done | bytes 49184 | tf_op jit(solution)/shard_map/ppermute | solution.py:345
  13.2 0.1 shard_map.125.refs_1_.refs_0_
  13.3 1.6 %collective-permute-start.3 = (bf16[16,6144]{1,0:T(8,128)(2,1)S(1)}, bf16[16,6144]{1,0:T(8,128)(2,1)S(1)}, u32[]{:S(2)}, u32[]{:S(2)}) collective-permute-start(bf16[16,6144]{1,0:T(8,128)(2,1)S(1)} %shard_map.125.refs_1_.refs_0_), channel_id=1, source_target_pairs={{0,2},{1,3},{2,0},{3,1},{4,6},{5,7},{6,4},{7,5},{8,10},{9,11},{10,... | collective-permute-start | bytes 589832 | tf_op jit(solution)/shard_map/ppermute | solution.py:345
  14.8 4.0 %shard_map.126.refs_1_.refs_5_ = bf16[2560,2048]{1,0:T(8,128)(2,1)S(1)} custom-call(bf16[6144,2048]{1,0:T(8,128)(2,1)} %refs_0_.3, bf16[16,6144]{1,0:T(8,128)(2,1)S(1)} %shard_map.125.refs_1_.refs_0_), custom_call_target="tpu_custom_call" | custom-call | bytes 10485760 | tf_op jit(solution)/shard_map/pallas_call | solution.py:80
  18.8 0.1 collective-permute-start.4
  18.9 0.1 collective-permute-done.3.refs_0_
  19.0 0.0 copy-start.6
  19.0 0.0 copy-start
  19.1 0.0 copy-start.3
  19.1 0.0 copy-start.4
  19.1 0.0 copy-start.5
  19.1 0.0 copy-start.2
  19.1 0.5 collective-permute-start.5
  19.6 0.8 %collective-permute-done.4.refs_2_ = bf16[16,6144]{1,0:T(8,128)(2,1)S(1)} collective-permute-done((bf16[16,6144]{1,0:T(8,128)(2,1)S(1)}, bf16[16,6144]{1,0:T(8,128)(2,1)S(1)}, u32[]{:S(2)}, u32[]{:S(2)}) %collective-permute-start.4) | collective-permute-done | bytes 196640 | tf_op jit(solution)/shard_map/ppermute | solution.py:345
  20.3 0.3 collective-permute-done.5.refs_3_
  20.6 16.2 %shard_map.128 = (f32[32,6144]{1,0:T(8,128)S(1)}, bf16[32,6144]{1,0:T(8,128)(2,1)S(1)}) custom-call(bf16[16,6144]{1,0:T(8,128)(2,1)S(1)} %shard_map.125.refs_1_.refs_0_, bf16[16,6144]{1,0:T(8,128)(2,1)S(1)} %shard_map.127.refs_1_, bf16[16,6144]{1,0:T(8,128)(2,1)S(1)} %collective-permute-done.4.refs_2_, bf16[16,6144]{1,0:T(8,128)(2,1)S(1)} %collective-permute-done.5.refs_3_, ...), custom_call_target="tpu_custom_call" | custom-call | flops 4831838208 | bytes 75497472 | tf_op jit(solution)/shard_map/pallas_call | solution.py:186
  36.9 0.4 collective-permute-start.6
  37.3 1.4 %collective-permute-done.6.received_ref = bf16[32,6144]{1,0:T(8,128)(2,1)S(1)} collective-permute-done((bf16[32,6144]{1,0:T(8,128)(2,1)S(1)}, bf16[32,6144]{1,0:T(8,128)(2,1)S(1)}, u32[]{:S(2)}, u32[]{:S(2)}) %collective-permute-start.6) | collective-permute-done | bytes 393248 | tf_op jit(solution)/shard_map/ppermute | solution.py:345
  38.7 0.1 shard_map.129
  38.7 1.5 %collective-permute-start.7 = (bf16[16,6144]{1,0:T(8,128)(2,1)S(1)}, bf16[16,6144]{1,0:T(8,128)(2,1)S(1)}, u32[]{:S(2)}, u32[]{:S(2)}) collective-permute-start(bf16[16,6144]{1,0:T(8,128)(2,1)S(1)} %get-tuple-element.16), channel_id=1, source_target_pairs={{0,2},{1,3},{2,0},{3,1},{4,6},{5,7},{6,4},{7,5},{8,10},{9,11},{10,... | collective-permute-start | bytes 589832 | tf_op jit(solution)/shard_map/ppermute | solution.py:345
  40.3 0.0 copy-done.6
  40.3 0.0 copy-done
  40.3 0.0 copy-done.3
  40.3 0.0 copy-done.4
  40.3 0.0 copy-start.1
  40.3 1.4 %copy-done.1 = bf16[4,192,1024]{2,1,0:T(8,128)(2,1)S(1)} copy-done((bf16[4,192,1024]{2,1,0:T(8,128)(2,1)S(1)}, bf16[4,192,1024]{2,1,0:T(8,128)(2,1)}, u32[]{:S(2)}) %copy-start.1) | copy-done | bytes 1572888
  41.7 3.6 %shard_map.122 = (bf16[4,6144]{1,0:T(4,128)(2,1)}, f32[8,128]{1,0:T(8,128)S(1)}) custom-call(s32[4]{0:T(128)S(1)} %copy-done.4, bf16[4,6144]{1,0:T(4,128)(2,1)S(1)} %copy-done.3, bf16[4,192,1024]{2,1,0:T(8,128)(2,1)S(1)} %copy-done, bf16[4,192,1024]{2,1,0:T(8,128)(2,1)S(1)} %copy-done.1), custom_call_target="tpu_custom_call" | custom-call | flops 150994944 | bytes 3145728 | tf_op jit(solution)/shard_map/pallas_call | solution.py:306
  45.3 0.7 %collective-permute-done.7.received_ref = bf16[16,6144]{1,0:T(8,128)(2,1)S(1)} collective-permute-done((bf16[16,6144]{1,0:T(8,128)(2,1)S(1)}, bf16[16,6144]{1,0:T(8,128)(2,1)S(1)}, u32[]{:S(2)}, u32[]{:S(2)}) %collective-permute-start.7) | collective-permute-done | bytes 196640 | tf_op jit(solution)/shard_map/ppermute | solution.py:345
  46.0 0.1 shard_map.130
  46.0 3.2 %collective-permute-start.10 = (bf16[4,6144]{1,0:T(4,128)(2,1)S(1)}, bf16[4,6144]{1,0:T(4,128)(2,1)S(1)}, u32[]{:S(2)}, u32[]{:S(2)}) collective-permute-start(bf16[4,6144]{1,0:T(4,128)(2,1)S(1)} %get-tuple-element.21), channel_id=1, source_target_pairs={{0,12},{1,13},{2,14},{3,15},{4,8},{5,9},{6,10},{7,11},{8,4},{9,5},... | collective-permute-start | bytes 147464 | tf_op jit(solution)/shard_map/ppermute | solution.py:345
  49.3 0.0 collective-permute-start.8
  49.3 1.2 %collective-permute-start.9 = (bf16[4,6144]{1,0:T(4,128)(2,1)S(1)}, bf16[4,6144]{1,0:T(4,128)(2,1)S(1)}, u32[]{:S(2)}, u32[]{:S(2)}) collective-permute-start(bf16[4,6144]{1,0:T(4,128)(2,1)S(1)} %get-tuple-element.20), channel_id=1, source_target_pairs={{0,8},{1,9},{2,10},{3,11},{4,12},{5,13},{6,14},{7,15},{8,0},{9,1},... | collective-permute-start | bytes 147464 | tf_op jit(solution)/shard_map/ppermute | solution.py:345
  50.5 0.0 copy-done.5
  50.5 0.1 select_reduce_fusion.coefficient_ref
  50.6 1.5 %collective-permute-done.10.refs_2_ = bf16[4,6144]{1,0:T(4,128)(2,1)S(1)} collective-permute-done((bf16[4,6144]{1,0:T(4,128)(2,1)S(1)}, bf16[4,6144]{1,0:T(4,128)(2,1)S(1)}, u32[]{:S(2)}, u32[]{:S(2)}) %collective-permute-start.10) | collective-permute-done | bytes 49184 | tf_op jit(solution)/shard_map/ppermute | solution.py:345
  52.1 1.3 %collective-permute-done.8.refs_0_ = bf16[4,6144]{1,0:T(4,128)(2,1)S(1)} collective-permute-done((bf16[4,6144]{1,0:T(4,128)(2,1)S(1)}, bf16[4,6144]{1,0:T(4,128)(2,1)S(1)}, u32[]{:S(2)}, u32[]{:S(2)}) %collective-permute-start.8) | collective-permute-done | bytes 49184 | tf_op jit(solution)/shard_map/ppermute | solution.py:345
  53.4 0.9 %collective-permute-done.9.refs_1_ = bf16[4,6144]{1,0:T(4,128)(2,1)S(1)} collective-permute-done((bf16[4,6144]{1,0:T(4,128)(2,1)S(1)}, bf16[4,6144]{1,0:T(4,128)(2,1)S(1)}, u32[]{:S(2)}, u32[]{:S(2)}) %collective-permute-start.9) | collective-permute-done | bytes 49184 | tf_op jit(solution)/shard_map/ppermute | solution.py:345
  54.3 0.0 copy-done.2
  54.3 0.8 %shard_map.131 = bf16[4,6144]{1,0:T(4,128)(2,1)} custom-call(bf16[4,6144]{1,0:T(4,128)(2,1)S(1)} %copy-done.2, f32[4,4]{1,0:T(4,128)S(1)} %select_reduce_fusion.coefficient_ref, f32[4,6144]{1,0:T(4,128)S(1)} %get-tuple-element.18.kept_ref, bf16[4,6144]{1,0:T(4,128)(2,1)S(1)} %collective-permute-done.8.refs_0_, ...), custom_call_target="tpu_custom_call" | custom-call | tf_op jit(solution)/shard_map/pallas_call | solution.py:263
  (3 shorter events, 0.0 us)
Async XLA Ops:
  1.6 10.9 %collective-permute-start = (bf16[4,6144]{1,0:T(4,128)(2,1)S(1)}, bf16[4,6144]{1,0:T(4,128)(2,1)S(1)}, u32[]{:S(2)}, u32[]{:S(2)}) collective-permute-start(bf16[4,6144]{1,0:T(4,128)(2,1)S(1)} %shard_map.123.refs_1_.refs_0_), channel_id=1, source_target_pairs={{0,4},{1,5},{2,6},{3,7},{4,0},{5,1},{6,2},{7,3},{8,12},{9,13},{10,... | collective-permute-start | bytes 147464 | tf_op jit(solution)/shard_map/ppermute | solution.py:345
  4.7 7.8 %collective-permute-start.1 = (bf16[4,6144]{1,0:T(4,128)(2,1)S(1)}, bf16[4,6144]{1,0:T(4,128)(2,1)S(1)}, u32[]{:S(2)}, u32[]{:S(2)}) collective-permute-start(bf16[4,6144]{1,0:T(4,128)(2,1)S(1)} %shard_map.123.refs_1_.refs_0_), channel_id=1, source_target_pairs={{0,8},{1,9},{2,10},{3,11},{4,12},{5,13},{6,14},{7,15},{8,0},{9,1},... | collective-permute-start | bytes 147464 | tf_op jit(solution)/shard_map/ppermute | solution.py:345
  7.3 5.9 %collective-permute-start.2 = (bf16[4,6144]{1,0:T(4,128)(2,1)S(1)}, bf16[4,6144]{1,0:T(4,128)(2,1)S(1)}, u32[]{:S(2)}, u32[]{:S(2)}) collective-permute-start(bf16[4,6144]{1,0:T(4,128)(2,1)S(1)} %shard_map.123.refs_1_.refs_0_), channel_id=1, source_target_pairs={{0,12},{1,13},{2,14},{3,15},{4,8},{5,9},{6,10},{7,11},{8,4},{9,5},... | collective-permute-start | bytes 147464 | tf_op jit(solution)/shard_map/ppermute | solution.py:345
  13.3 5.7 %collective-permute-start.3 = (bf16[16,6144]{1,0:T(8,128)(2,1)S(1)}, bf16[16,6144]{1,0:T(8,128)(2,1)S(1)}, u32[]{:S(2)}, u32[]{:S(2)}) collective-permute-start(bf16[16,6144]{1,0:T(8,128)(2,1)S(1)} %shard_map.125.refs_1_.refs_0_), channel_id=1, source_target_pairs={{0,2},{1,3},{2,0},{3,1},{4,6},{5,7},{6,4},{7,5},{8,10},{9,11},{10,... | collective-permute-start | bytes 589832 | tf_op jit(solution)/shard_map/ppermute | solution.py:345
  18.8 1.5 %collective-permute-start.4 = (bf16[16,6144]{1,0:T(8,128)(2,1)S(1)}, bf16[16,6144]{1,0:T(8,128)(2,1)S(1)}, u32[]{:S(2)}, u32[]{:S(2)}) collective-permute-start(bf16[16,6144]{1,0:T(8,128)(2,1)S(1)} %shard_map.125.refs_1_.refs_0_), channel_id=1, source_target_pairs={{0,1},{1,0},{2,3},{3,2},{4,5},{5,4},{6,7},{7,6},{8,9},{9,8},{10,11... | collective-permute-start | bytes 589832 | tf_op jit(solution)/shard_map/ppermute | solution.py:345
  19.0 21.3 %copy-start.6 = (bf16[4,2]{0,1:T(2,128)(2,1)S(1)}, bf16[4,2]{0,1:T(2,128)(2,1)}, u32[]{:S(2)}) copy-start(bf16[4,2]{0,1:T(2,128)(2,1)} %param.18) | copy-start | bytes 52
  19.0 21.2 %copy-start = (bf16[4,192,1024]{2,1,0:T(8,128)(2,1)S(1)}, bf16[4,192,1024]{2,1,0:T(8,128)(2,1)}, u32[]{:S(2)}) copy-start(bf16[4,192,1024]{2,1,0:T(8,128)(2,1)} %keys_ref.1) | copy-start | bytes 4718596
  19.1 21.2 %copy-start.3 = (bf16[4,6144]{1,0:T(4,128)(2,1)S(1)}, bf16[4,6144]{1,0:T(4,128)(2,1)}, u32[]{:S(2)}) copy-start(bf16[4,6144]{1,0:T(4,128)(2,1)} %queries_ref.1) | copy-start | bytes 147460
  19.1 21.2 %copy-start.4 = (s32[4]{0:T(128)S(1)}, s32[4]{0:T(128)}, u32[]{:S(2)}) copy-start(s32[4]{0:T(128)} %lengths_ref.1) | copy-start | bytes 52
  19.1 31.4 %copy-start.5 = (s32[4,2]{0,1:T(2,128)S(1)}, s32[4,2]{0,1:T(2,128)}, u32[]{:S(2)}) copy-start(s32[4,2]{0,1:T(2,128)} %param.17) | copy-start | bytes 100
  19.1 35.2 %copy-start.2 = (bf16[4,6144]{1,0:T(4,128)(2,1)S(1)}, bf16[4,6144]{1,0:T(4,128)(2,1)}, u32[]{:S(2)}) copy-start(bf16[4,6144]{1,0:T(4,128)(2,1)} %hidden_ref.1) | copy-start | bytes 147460
  19.1 1.5 %collective-permute-start.5 = (bf16[16,6144]{1,0:T(8,128)(2,1)S(1)}, bf16[16,6144]{1,0:T(8,128)(2,1)S(1)}, u32[]{:S(2)}, u32[]{:S(2)}) collective-permute-start(bf16[16,6144]{1,0:T(8,128)(2,1)S(1)} %shard_map.127.refs_1_), channel_id=1, source_target_pairs={{0,1},{1,0},{2,3},{3,2},{4,5},{5,4},{6,7},{7,6},{8,9},{9,8},{10,11... | collective-permute-start | bytes 589832 | tf_op jit(solution)/shard_map/ppermute | solution.py:345
  36.9 1.8 %collective-permute-start.6 = (bf16[32,6144]{1,0:T(8,128)(2,1)S(1)}, bf16[32,6144]{1,0:T(8,128)(2,1)S(1)}, u32[]{:S(2)}, u32[]{:S(2)}) collective-permute-start(bf16[32,6144]{1,0:T(8,128)(2,1)S(1)} %get-tuple-element.14), channel_id=1, source_target_pairs={{0,1},{1,0},{2,3},{3,2},{4,5},{5,4},{6,7},{7,6},{8,9},{9,8},{10,11... | collective-permute-start | bytes 1179656 | tf_op jit(solution)/shard_map/ppermute | solution.py:345
  38.7 7.2 %collective-permute-start.7 = (bf16[16,6144]{1,0:T(8,128)(2,1)S(1)}, bf16[16,6144]{1,0:T(8,128)(2,1)S(1)}, u32[]{:S(2)}, u32[]{:S(2)}) collective-permute-start(bf16[16,6144]{1,0:T(8,128)(2,1)S(1)} %get-tuple-element.16), channel_id=1, source_target_pairs={{0,2},{1,3},{2,0},{3,1},{4,6},{5,7},{6,4},{7,5},{8,10},{9,11},{10,... | collective-permute-start | bytes 589832 | tf_op jit(solution)/shard_map/ppermute | solution.py:345
  40.3 1.4 %copy-start.1 = (bf16[4,192,1024]{2,1,0:T(8,128)(2,1)S(1)}, bf16[4,192,1024]{2,1,0:T(8,128)(2,1)}, u32[]{:S(2)}) copy-start(bf16[4,192,1024]{2,1,0:T(8,128)(2,1)} %values_ref.1) | copy-start | bytes 4718596
  46.0 6.0 %collective-permute-start.10 = (bf16[4,6144]{1,0:T(4,128)(2,1)S(1)}, bf16[4,6144]{1,0:T(4,128)(2,1)S(1)}, u32[]{:S(2)}, u32[]{:S(2)}) collective-permute-start(bf16[4,6144]{1,0:T(4,128)(2,1)S(1)} %get-tuple-element.21), channel_id=1, source_target_pairs={{0,12},{1,13},{2,14},{3,15},{4,8},{5,9},{6,10},{7,11},{8,4},{9,5},... | collective-permute-start | bytes 147464 | tf_op jit(solution)/shard_map/ppermute | solution.py:345
  49.3 4.1 %collective-permute-start.8 = (bf16[4,6144]{1,0:T(4,128)(2,1)S(1)}, bf16[4,6144]{1,0:T(4,128)(2,1)S(1)}, u32[]{:S(2)}, u32[]{:S(2)}) collective-permute-start(bf16[4,6144]{1,0:T(4,128)(2,1)S(1)} %get-tuple-element.19), channel_id=1, source_target_pairs={{0,4},{1,5},{2,6},{3,7},{4,0},{5,1},{6,2},{7,3},{8,12},{9,13},{10,... | collective-permute-start | bytes 147464 | tf_op jit(solution)/shard_map/ppermute | solution.py:345
  49.3 5.0 %collective-permute-start.9 = (bf16[4,6144]{1,0:T(4,128)(2,1)S(1)}, bf16[4,6144]{1,0:T(4,128)(2,1)S(1)}, u32[]{:S(2)}, u32[]{:S(2)}) collective-permute-start(bf16[4,6144]{1,0:T(4,128)(2,1)S(1)} %get-tuple-element.20), channel_id=1, source_target_pairs={{0,8},{1,9},{2,10},{3,11},{4,12},{5,13},{6,14},{7,15},{8,0},{9,1},... | collective-permute-start | bytes 147464 | tf_op jit(solution)/shard_map/ppermute | solution.py:345
